TPU v7x, 32 devices: a whole 2x2x4 slice. The times are simulated.
32 devices in a mesh: ptg: 4 (over z), img: 8 (over y, x, core).
Axes of the slice: x: 2, y: 2, z: 4, core: 2. Of those that a mesh axis runs over, the one named last changes fastest.
Arguments:
- image: bfloat16 [2048, 4096], P(None, 'img'), may hold values from -6 to 6
- beam: float32 [4, 2048, 2048], P('ptg', 'img'), may hold values from 0.2 to 1
- counts: int32 [4, 2048, 2048], P('ptg', None, 'img'), may hold values from 0 to 15
- offsets: int32 [4], P('ptg'), may hold values from 0 to 2048, as said below
Outputs:
- hessian_image: float32 [2048, 4096], P('ptg', 'img')
Inputs may be any that keep to these rules, and one draw needn't show every extreme that they name: offsets rise with the pointing; the first is 0 and the last is 2048.
All inputs are finite; a program needn't handle non-finite values.
Results may differ from a plain program's by a relative error of at most 0.0095.
Values may be sent and summed in bfloat16 or wider, within the bound.
A program may use at most 64 MiB of HBM per device.

v0:
```python
import math

import jax
import jax.numpy as jnp
from jax import lax
from jax.sharding import PartitionSpec as P


def tables(points):
    index_row = jnp.arange(points, dtype=jnp.int32)
    phase = index_row[:, None] * index_row[None, :] % points
    angle = phase.astype(jnp.float32) * (2.0 * math.pi / points)
    return (jnp.cos(angle).astype(jnp.bfloat16), (-jnp.sin(angle)).astype(jnp.bfloat16))


def shards(image, beam, counts, offsets):
    points = counts.shape[1]
    start = offsets[0]
    cosine, sine_table = tables(points)
    strip = lax.all_to_all(image, "img", split_axis=0, concat_axis=1, tiled=True)
    window = lax.dynamic_slice_in_dim(strip, start, points, 1)
    beamed = (beam[0] * window.astype(jnp.float32)).astype(jnp.bfloat16)
    row_real = jnp.dot(beamed, cosine, preferred_element_type=jnp.float32).astype(jnp.bfloat16)
    row_imag = jnp.dot(beamed, sine_table, preferred_element_type=jnp.float32).astype(jnp.bfloat16)
    col_real, col_imag = (
        lax.all_to_all(row_real, "img", split_axis=1, concat_axis=0, tiled=True),
        lax.all_to_all(row_imag, "img", split_axis=1, concat_axis=0, tiled=True),
    )
    spec_real = jnp.dot(cosine, col_real, preferred_element_type=jnp.float32) - jnp.dot(
        sine_table, col_imag, preferred_element_type=jnp.float32
    )
    spec_imag = jnp.dot(sine_table, col_real, preferred_element_type=jnp.float32) + jnp.dot(
        cosine, col_imag, preferred_element_type=jnp.float32
    )
    weight = counts[0].astype(jnp.float32) / float(points * points)
    weighted_real = (weight * spec_real).astype(jnp.bfloat16)
    weighted_imag = (weight * spec_imag).astype(jnp.bfloat16)
    back_real = (
        jnp.dot(cosine, weighted_real, preferred_element_type=jnp.float32)
        + jnp.dot(sine_table, weighted_imag, preferred_element_type=jnp.float32)
    ).astype(jnp.bfloat16)
    back_imag = (
        jnp.dot(cosine, weighted_imag, preferred_element_type=jnp.float32)
        - jnp.dot(sine_table, weighted_real, preferred_element_type=jnp.float32)
    ).astype(jnp.bfloat16)
    rows_real, rows_imag = (
        lax.all_to_all(back_real, "img", split_axis=0, concat_axis=1, tiled=True),
        lax.all_to_all(back_imag, "img", split_axis=0, concat_axis=1, tiled=True),
    )
    image_real = jnp.dot(rows_real, cosine, preferred_element_type=jnp.float32) + jnp.dot(
        rows_imag, sine_table, preferred_element_type=jnp.float32
    )
    contribution = (beam[0] * image_real).astype(jnp.bfloat16)
    placed = lax.dynamic_update_slice_in_dim(
        jnp.zeros((contribution.shape[0], strip.shape[1]), jnp.bfloat16), contribution, start, 1
    )
    tile_terms = lax.all_to_all(placed, "img", split_axis=1, concat_axis=0, tiled=True).astype(
        jnp.float32
    )
    summed = lax.psum(tile_terms.astype(jnp.bfloat16), "ptg").astype(jnp.float32)
    share_rows = summed.shape[0] // lax.axis_size("ptg")
    return lax.dynamic_slice_in_dim(summed, lax.axis_index("ptg") * share_rows, share_rows, 0)


def solution(mesh):
    return jax.shard_map(
        shards,
        mesh=mesh,
        in_specs=(P(None, "img"), P("ptg", "img", None), P("ptg", None, "img"), P("ptg")),
        out_specs=P("ptg", "img"),
        check_vma=False,
    )
```

profile of v0, /device:TPU:1, one launch (start us, length us, event | category | flops | bytes accessed | tf_op | source)
XLA Modules:
  0.0 1026.3 jit_solution(1970597806490351236)
XLA Ops:
  6.5 5.2 all-to-all-start
  12.4 22.5 %all-to-all-done = bf16[8,256,512]{2,1,0:T(8,128)(2,1)S(1)} async-done(((bf16[8,256,512]{2,1,0:T(8,128)(2,1)}), bf16[8,256,512]{2,1,0:T(8,128)(2,1)S(1)}, u32[]{:S(2)}, u32[]{:S(2)}) %all-to-all-start) | async-done | bytes 2097184 | tf_op jit(solution)/shard_map/all_to_all | solution.py:20
  35.0 0.3 copy.28
  35.2 1.3 copy-done
  36.5 0.6 fusion.33
  37.1 62.9 %fusion.32 = bf16[256,2048]{1,0:T(8,128)(2,1)S(1)} fusion(bf16[256,2048]{1,0:T(8,128)(2,1)S(1)} %fusion.33), kind=kOutput, calls=%fused_computation.37 | convolution fusion | flops 2210922496 | bytes 2097152 | tf_op jit(solution)/shard_map/dot_general | solution.py:23
  100.0 1.0 copy.32
  101.1 7.2 all-to-all-start.1
  108.2 63.9 %fusion.31 = bf16[256,2048]{1,0:T(8,128)(2,1)S(1)} fusion(bf16[256,2048]{1,0:T(8,128)(2,1)S(1)} %fusion.33), kind=kOutput, calls=%fused_computation.36 | convolution fusion | flops 2215116800 | bytes 2097152 | tf_op jit(solution)/shard_map/dot_general | solution.py:24
  172.1 1.0 copy.31
  173.2 4.5 all-to-all-start.2
  177.7 71.5 %fusion.10 = f32[2048,256]{1,0:T(8,128)} fusion(bf16[2048,256]{1,0:T(8,128)(2,1)S(1)} %bitcast.71), kind=kOutput, calls=%fused_computation.15 | convolution fusion | flops 2210398208 | bytes 3145728 | tf_op jit(solution)/shard_map/dot_general | solution.py:29
  249.2 70.7 %fusion.8 = f32[2048,256]{1,0:T(8,128)S(1)} fusion(bf16[2048,256]{1,0:T(8,128)(2,1)S(1)} %bitcast.74), kind=kOutput, calls=%fused_computation.13 | convolution fusion | flops 2210398208 | bytes 3145728 | tf_op jit(solution)/shard_map/dot_general | solution.py:32
  319.9 72.0 %fusion.30 = bf16[2048,256]{1,0:T(8,128)(2,1)S(1)} fusion(f32[2048,256]{1,0:T(8,128)S(1)} %copy-done.3, bf16[2048,256]{1,0:T(8,128)(2,1)S(1)} %bitcast.75, s32[1,2048,256]{2,1,0:T(8,128)S(1)} %copy-done.2), kind=kOutput, calls=%fused_computation.35 | convolution fusion | flops 2217213952 | bytes 6291456 | tf_op jit(solution)/shard_map/dot_general | solution.py:29
  391.8 72.0 %fusion.29 = bf16[2048,256]{1,0:T(8,128)(2,1)S(1)} fusion(f32[2048,256]{1,0:T(8,128)S(1)} %fusion.8, bf16[2048,256]{1,0:T(8,128)(2,1)S(1)} %bitcast.72, s32[1,2048,256]{2,1,0:T(8,128)S(1)} %copy-done.2), kind=kOutput, calls=%fused_computation.34 | convolution fusion | flops 2217213952 | bytes 6291456 | tf_op jit(solution)/shard_map/dot_general | solution.py:32
  463.8 71.5 %fusion.6 = f32[2048,256]{1,0:T(8,128)} fusion(bf16[2048,256]{1,0:T(8,128)(2,1)S(1)} %fusion.29), kind=kOutput, calls=%fused_computation.11 | convolution fusion | flops 2210398208 | bytes 3145728 | tf_op jit(solution)/shard_map/dot_general | solution.py:43
  535.3 70.6 %fusion.9 = f32[2048,256]{1,0:T(8,128)S(1)} fusion(bf16[2048,256]{1,0:T(8,128)(2,1)S(1)} %fusion.30), kind=kOutput, calls=%fused_computation.14 | convolution fusion | flops 2210398208 | bytes 3145728 | tf_op jit(solution)/shard_map/dot_general | solution.py:39
  605.9 71.9 %fusion.28 = bf16[2048,256]{1,0:T(8,128)(2,1)S(1)} fusion(f32[2048,256]{1,0:T(8,128)S(1)} %fusion.9, bf16[2048,256]{1,0:T(8,128)(2,1)S(1)} %fusion.29), kind=kOutput, calls=%fused_computation.33 | convolution fusion | flops 2215641088 | bytes 4194304 | tf_op jit(solution)/shard_map/dot_general | solution.py:40
  677.8 1.3 copy.22
  679.2 4.2 all-to-all-start.3
  683.4 72.7 %fusion.27 = bf16[2048,256]{1,0:T(8,128)(2,1)S(1)} fusion(f32[2048,256]{1,0:T(8,128)} %fusion.6, bf16[2048,256]{1,0:T(8,128)(2,1)S(1)} %fusion.30), kind=kOutput, calls=%fused_computation.32 | convolution fusion | flops 2215641088 | bytes 4194304 | tf_op jit(solution)/shard_map/dot_general | solution.py:44
  756.1 1.3 copy.23
  757.4 4.2 all-to-all-start.4
  761.6 0.5 all-reduce.2.cloned.1.call-start
  762.1 63.0 %fusion.7 = f32[256,2048]{1,0:T(8,128)} fusion(bf16[256,2048]{0,1:T(8,128)(2,1)S(1)} %bitcast.73), kind=kOutput, calls=%fused_computation.12 | convolution fusion | flops 2210398208 | bytes 3145728 | tf_op jit(solution)/shard_map/dot_general | solution.py:50
  825.2 66.4 %fusion.26 = bf16[256,2048]{1,0:T(8,128)(2,1)S(1)} fusion(f32[256,2048]{1,0:T(8,128)} %fusion.7, bf16[256,2048]{0,1:T(8,128)(2,1)} %bitcast.16, f32[1,256,2048]{2,1,0:T(8,128)S(1)} %copy-done.1), kind=kOutput, calls=%fused_computation.31 | convolution fusion | flops 2216165376 | bytes 6291456 | tf_op jit(solution)/shard_map/dot_general | solution.py:50
  891.6 0.5 copy.24
  892.3 5.3 dynamic_update_slice.3
  897.6 29.4 %all_to_all.114 = bf16[256,8,512]{0,2,1:T(8,128)(2,1)} all-to-all(bf16[256,8,512]{0,2,1:T(8,128)(2,1)S(1)} %bitcast.67), channel_id=1, replica_groups=mesh['ptg'=4,'img'=8] {'img'}, dimensions={1} | all-to-all | bytes 4194304 | tf_op jit(solution)/shard_map/all_to_all | solution.py:57
  926.9 3.9 copy.25
  930.9 86.3 %all-reduce.2.cloned.1.call-done = bf16[2048,512]{1,0:T(8,128)(2,1)} async-done(((bf16[2048,512]{1,0:T(8,128)(2,1)}), bf16[2048,512]{1,0:T(8,128)(2,1)}) %all-reduce.2.cloned.1.call-update) | async-done | bytes 2097168 | tf_op jit(solution)/shard_map/psum | solution.py:60
  1017.2 2.1 dynamic-slice_convert_fusion
  (13 shorter events, 0.2 us)
Async XLA Ops:
  6.5 28.4 %all-to-all-start = ((bf16[8,256,512]{2,1,0:T(8,128)(2,1)}), bf16[8,256,512]{2,1,0:T(8,128)(2,1)S(1)}, u32[]{:S(2)}, u32[]{:S(2)}) async-start(bf16[8,256,512]{2,1,0:T(8,128)(2,1)} %bitcast.70), calls=%async_computation | async-start | bytes 4194304 | tf_op jit(solution)/shard_map/all_to_all | solution.py:20
  35.0 1.6 copy-start
  101.1 72.1 %all-to-all-start.1 = ((bf16[256,8,256]{2,0,1:T(8,128)(2,1)}), bf16[256,8,256]{2,0,1:T(8,128)(2,1)S(1)}, u32[]{:S(2)}, u32[]{:S(2)}) async-start(bf16[256,8,256]{2,0,1:T(8,128)(2,1)} %bitcast.61), calls=%async_computation.1 | async-start | bytes 2097152 | tf_op jit(solution)/shard_map/all_to_all | solution.py:26
  173.2 76.0 %all-to-all-start.2 = ((bf16[256,8,256]{2,0,1:T(8,128)(2,1)}), bf16[256,8,256]{2,0,1:T(8,128)(2,1)S(1)}, u32[]{:S(2)}, u32[]{:S(2)}) async-start(bf16[256,8,256]{2,0,1:T(8,128)(2,1)} %bitcast.60), calls=%async_computation.2 | async-start | bytes 2097152 | tf_op jit(solution)/shard_map/all_to_all | solution.py:27
  249.2 70.7 %copy-start.2 = (s32[1,2048,256]{2,1,0:T(8,128)S(1)}, s32[1,2048,256]{2,1,0:T(8,128)}, u32[]{:S(2)}) copy-start(s32[1,2048,256]{2,1,0:T(8,128)} %param.6) | copy-start | bytes 6291460
  249.2 70.7 %copy-start.3 = (f32[2048,256]{1,0:T(8,128)S(1)}, f32[2048,256]{1,0:T(8,128)}, u32[]{:S(2)}) copy-start(f32[2048,256]{1,0:T(8,128)} %fusion.10) | copy-start | bytes 6291460
  679.2 78.2 %all-to-all-start.3 = ((bf16[8,256,256]{1,2,0:T(8,128)(2,1)}), bf16[8,256,256]{1,2,0:T(8,128)(2,1)S(1)}, u32[]{:S(2)}, u32[]{:S(2)}) async-start(bf16[8,256,256]{1,2,0:T(8,128)(2,1)} %copy.22), calls=%async_computation.3 | async-start | bytes 2097152 | tf_op jit(solution)/shard_map/all_to_all | solution.py:47
  757.4 67.8 %all-to-all-start.4 = ((bf16[8,256,256]{1,2,0:T(8,128)(2,1)}), bf16[8,256,256]{1,2,0:T(8,128)(2,1)}, u32[]{:S(2)}, u32[]{:S(2)}) async-start(bf16[8,256,256]{1,2,0:T(8,128)(2,1)} %copy.23), calls=%async_computation.4 | async-start | bytes 2097152 | tf_op jit(solution)/shard_map/all_to_all | solution.py:48
  761.6 255.6 %all-reduce.2.cloned.1.call-start = ((), (), s32[]{:S(2)}) async-start(), calls=%async_computation.6 | async-start | bytes 4194304 | tf_op jit(solution)/shard_map/psum | solution.py:60
  762.1 63.1 %copy-start.1 = (f32[1,256,2048]{2,1,0:T(8,128)S(1)}, f32[1,256,2048]{2,1,0:T(8,128)}, u32[]{:S(2)}) copy-start(f32[1,256,2048]{2,1,0:T(8,128)} %param.5) | copy-start | bytes 6291460
Sparse Core Ops, SparseCore 0:
  931.0 86.1 all-reduce.1
where the time goes:
time: 1030 us
  matrix products  829 us (80%)
  waiting for transfers between devices  109 us (11%)
  blocking collectives  29.4 us (3%)
  starting transfers between devices  25.8 us (3%)
  local copies, waits for them, and re-layouts  16.2 us (2%)
  between operations  14.4 us (1%)
    psum x1, waiting for transfers between devices, shards(): lax.psum(tile_terms.astype(jnp.bfloat16), 'ptg').astype(jnp.float32)  86.3 us
    dot_general x1, matrix products, shards(): jnp.dot(sine_table, weighted_real, preferred_element_type=jnp.float32)  72.7 us
    dot_general x1, matrix products, shards(): jnp.dot(sine_table, col_imag, preferred_element_type=jnp.float32)  72 us
    dot_general x1, matrix products, shards(): jnp.dot(sine_table, col_real, preferred_element_type=jnp.float32)  72 us
    dot_general x1, matrix products, shards(): jnp.dot(sine_table, weighted_imag, preferred_element_type=jnp.float32)  71.9 us
    dot_general x1, matrix products, shards(): jnp.dot(cosine, weighted_imag, preferred_element_type=jnp.float32)  71.5 us
    dot_general x1, matrix products, shards(): jnp.dot(cosine, col_real, preferred_element_type=jnp.float32)  71.5 us
    dot_general x1, matrix products, shards(): jnp.dot(cosine, col_imag, preferred_element_type=jnp.float32)  70.7 us
  transfers between devices with their start and end apart: 6, of which 2 were waited for; matrix products, arithmetic and copies ran while one was open for 27% of the time, Pallas kernels for 0%

commit v1 on v0

v1 whole, which is shorter than its diff:
```python
import jax
import jax.numpy as jnp
import ml_dtypes
import numpy as np
from jax import lax
from jax.sharding import PartitionSpec as P

BF = ml_dtypes.bfloat16


def slots_of(points, parts):
    wide = points // parts
    half = wide // 2
    rows = []
    for d in range(parts):
        first = wide * d + (0 if d < parts // 2 else 1)
        rows.append(np.arange(first, first + half))
    return np.stack(rows)


def make_tables(points, parts):
    index = np.arange(points, dtype=np.int64)
    angle = 2.0 * np.pi / points * np.arange(points)
    cos_of, sin_of = np.cos(angle), -np.sin(angle)
    phase = index[:, None] * index[None, :] % points
    column = np.concatenate([cos_of[phase], sin_of[phase]], 0).astype(BF)
    slots = slots_of(points, parts)
    blocks = []
    for d in range(parts):
        phase = index[:, None] * slots[d][None, :] % points
        real, imag = cos_of[phase], sin_of[phase]
        if d == 0:
            imag[:, 0] = 1.0 - 2.0 * (index % 2)
        blocks += [real, imag]
    return column, np.concatenate(blocks, 1).astype(BF)


def make_selectors(points, parts):
    wide = points // parts
    half = wide // 2
    send = np.zeros((parts, wide, half), BF)
    own = np.zeros((parts, wide, wide), BF)
    mirror_own = np.zeros((parts, wide, wide), BF)
    mirror_recv = np.zeros((parts, half, wide), BF)
    mirror_col = np.zeros((parts, 8, wide), BF)
    own_col = np.zeros((parts, 8, wide), BF)
    scale = np.full((parts, 1, wide), 1.0 / float(points * points), np.float32)
    for d in range(parts):
        low = d < parts // 2
        for j in range(half):
            if low:
                send[d, wide - 1 - j, j] = 1
                own[d, j, j] = own[d, j, half + j] = 1
            else:
                if j:
                    send[d, wide - j, j] = 1
                own[d, j + 1, j] = own[d, j + 1, half + j] = 1
            if j or not low:
                mirror_recv[d, j, j] = mirror_recv[d, j, half + j] = 1
        if d == 0:
            own[d, 0, half] = 0
            mirror_own[d, 0, 0] = 1
            own_col[d, 0, half] = mirror_col[d, 0, half] = 1
            scale[d, 0, 0] = scale[d, 0, half] = 0.5 / float(points * points)
        elif low:
            mirror_col[d, 0, 0] = mirror_col[d, 0, half] = 1
    return send, own, mirror_own, mirror_recv, mirror_col, own_col, scale


def dot(a, b, dims=((1,), (0,))):
    return lax.dot_general(a, b, (dims, ((), ())), preferred_element_type=jnp.float32)


def weights(counts, points, parts):
    me = lax.axis_index("img")
    send, own, mirror_own, mirror_recv, mirror_col, own_col, scale = (
        jnp.asarray(a)[me] for a in make_selectors(points, parts)
    )
    values = counts.astype(jnp.bfloat16)
    sent = dot(values, send).astype(jnp.bfloat16)
    pairs = [(d, parts - 1 - d) for d in range(parts)]
    recv = lax.ppermute(sent, "img", pairs)
    first = np.zeros((8, points // parts), BF)
    first[0, 0] = 1
    column = dot(jnp.asarray(first), values, ((1,), (1,))).astype(jnp.bfloat16)
    pairs = [(parts // 2, 0)] + [(parts - d, d) for d in range(1, parts // 2)]
    column = lax.ppermute(column, "img", pairs)
    mirror = dot(recv, mirror_recv) + dot(values, mirror_own) + dot(column, mirror_col, ((0,), (0,)))
    index = jnp.arange(points, dtype=jnp.int32)
    flip = ((index[:, None] + index[None, :]) % points == 0).astype(jnp.bfloat16)
    total = dot(values, own) + dot(column, own_col, ((0,), (0,))) + dot(flip, mirror.astype(jnp.bfloat16))
    return total * scale


def shards(image, beam, counts, offsets):
    points = counts.shape[1]
    parts, layers = lax.axis_size("img"), lax.axis_size("ptg")
    me, layer = lax.axis_index("img"), lax.axis_index("ptg")
    tile = image.shape[1]
    folds = tile * parts // points
    rows = points // parts
    wide, half = points // parts, points // parts // 2
    chunk = points // layers
    start = offsets[0]
    table_np, row_np = make_tables(points, parts)
    table, row_table = jnp.asarray(table_np), jnp.asarray(row_np)

    strip = lax.all_to_all(image, "img", split_axis=0, concat_axis=1, tiled=True)
    starts = lax.all_gather(offsets, "ptg", tiled=True)
    weight = weights(counts[0], points, parts)
    shift = start % points
    twice = jnp.concatenate([beam[0], beam[0]], 1)
    rolled = lax.dynamic_slice_in_dim(twice, points - shift, points, 1)

    place = jnp.arange(points, dtype=jnp.int32)
    window = strip[:, (folds - 1) * points :]
    for f in range(folds - 2, -1, -1):
        window = jnp.where(place + f * points >= start, strip[:, f * points : (f + 1) * points], window)
    beamed = (rolled * window.astype(jnp.float32)).astype(jnp.bfloat16)
    row = dot(beamed, row_table).astype(jnp.bfloat16)
    col = lax.all_to_all(row, "img", split_axis=1, concat_axis=0, tiled=True)
    spec = dot(table, col)
    c_re, c_im = spec[:points, :half], spec[:points, half:]
    s_re, s_im = spec[points:, :half], spec[points:, half:]
    packed = (jnp.arange(half) == 0) & (me == 0)
    real, imag = c_re - s_im, s_re + c_im
    upper = jnp.concatenate([jnp.where(packed, c_re, real), jnp.where(packed, c_im, imag)], 1)
    lower = jnp.concatenate([jnp.where(packed, s_re, imag), jnp.where(packed, s_im, -real)], 1)
    weighted = jnp.concatenate([weight * upper, weight * lower], 0).astype(jnp.bfloat16)
    back = dot(table, weighted, ((0,), (0,))).astype(jnp.bfloat16)
    rows_back = lax.all_to_all(back, "img", split_axis=0, concat_axis=1, tiled=True)
    contribution = (rolled * dot(rows_back, row_table, ((1,), (1,)))).astype(jnp.bfloat16)
    terms = lax.all_to_all(contribution, "ptg", split_axis=1, concat_axis=0, tiled=True)
    terms = terms.reshape(layers, rows, chunk).astype(jnp.float32)

    at = layer * chunk + jnp.arange(chunk, dtype=jnp.int32)
    sums = []
    for f in range(folds):
        inside = (at + f * points >= starts[:, None]) & (at + f * points < starts[:, None] + points)
        sums.append(jnp.sum(jnp.where(inside[:, None, :], terms, 0.0), 0).astype(jnp.bfloat16))
    sums = jnp.stack(sums)

    out_rows = points // layers
    tall, broad = out_rows // rows, tile // chunk
    out = jnp.zeros((out_rows, tile), jnp.float32)
    for s in range(folds):
        pairs = []
        row_at = np.zeros((layers * parts,), np.int32)
        col_at = np.zeros((layers * parts,), np.int32)
        for p in range(layers):
            for i in range(parts):
                f = (i % tall * broad + p % broad + s) % folds
                q, c = i * rows // out_rows, (points * f + chunk * p) // tile
                pairs.append((p * parts + i, q * parts + c))
                row_at[q * parts + c] = i * rows - q * out_rows
                col_at[q * parts + c] = points * f + chunk * p - tile * c
        piece = lax.dynamic_index_in_dim(sums, (me % tall * broad + layer % broad + s) % folds, 0, False)
        piece = lax.ppermute(piece, ("ptg", "img"), pairs)
        here = layer * parts + me
        out = lax.dynamic_update_slice(
            out, piece.astype(jnp.float32), (jnp.asarray(row_at)[here], jnp.asarray(col_at)[here])
        )
    return out


def solution(mesh):
    return jax.shard_map(
        shards,
        mesh=mesh,
        in_specs=(P(None, "img"), P("ptg", "img", None), P("ptg", None, "img"), P("ptg")),
        out_specs=P("ptg", "img"),
        check_vma=False,
    )
```

time: 1030 us -> 189 us (0.18)
  matrix products: 829 us -> 50.2 us
  waiting for transfers between devices: 109 us -> 43 us
  blocking collectives: 29.4 us -> 44.1 us
    dot_general x12, matrix products: 829 us -> 50.2 us  [dot(): lax.dot_general(a, b, (dims, ((), ())), preferred_element_type=jnp.float32)]
    psum x1 -> x0, waiting for transfers between devices: 86.3 us -> none  [shards(): lax.psum(tile_terms.astype(jnp.bfloat16), 'ptg').astype(jnp.float32)]
    ppermute x0 -> x4, waiting for transfers between devices: none -> 41.4 us  [the longest x2 28.6 us: shards(): piece = lax.ppermute(piece, ('ptg', 'img'), pairs)]
    unnamed x0 -> x1, blocking collectives: none -> 24.1 us
    all_to_all x1, waiting for transfers between devices: 22.5 us -> 0.01 us  [shards(): lax.all_to_all(image, 'img', split_axis=0, concat_axis=1, tiled=True)]
  transfers between devices with their start and end apart: 6 -> 7, of which waited for: 2 -> 4; matrix products, arithmetic and copies ran while one was open for 27% -> 17% of each run, Pallas kernels for 0% -> 0%
where the time goes in v1:
time: 189 us; the launch traced here: 188 us
  matrix products  50.2 us (27%)
  blocking collectives  44.1 us (23%)
  waiting for transfers between devices  43 us (23%)
  starting transfers between devices  33.1 us (18%)
  local copies, waits for them, and re-layouts  8.33 us (4%)
  other arithmetic  4.87 us (3%)
  between operations  4.76 us (3%)
    dot_general x12, matrix products, dot(): lax.dot_general(a, b, (dims, ((), ())), preferred_element_type=jnp.float32)  50.2 us
    ppermute x2, waiting for transfers between devices, shards(): piece = lax.ppermute(piece, ('ptg', 'img'), pairs)  28.6 us
    unnamed x1, blocking collectives  24.1 us
    all_to_all x1, blocking collectives, shards(): lax.all_to_all(back, 'img', split_axis=0, concat_axis=1, tiled=True)  20 us
    all_to_all x1, starting transfers between devices, shards(): col = lax.all_to_all(row, 'img', split_axis=1, concat_axis=0, tiled=True)  13.8 us
    ppermute x1, waiting for transfers between devices, weights(): column = lax.ppermute(column, 'img', pairs)  12.8 us
    all_to_all x1, starting transfers between devices, shards(): lax.all_to_all(image, 'img', split_axis=0, concat_axis=1, tiled=True)  5.35 us
    all_to_all x1, starting transfers between devices, shards(): lax.all_to_all(contribution, 'ptg', split_axis=1, concat_axis=0, tiled=True)  5.26 us
  transfers between devices with their start and end apart: 7, of which 4 were waited for; matrix products, arithmetic and copies ran while one was open for 17% of the time, Pallas kernels for 0%

profile of v1, /device:TPU:1, one launch (start us, length us, event | category | flops | bytes accessed | tf_op | source)
XLA Modules:
  0.0 188.4 jit_solution(13477312802999015891)
XLA Ops:
  0.0 5.4 %all-to-all-start = ((bf16[8,256,512]{2,1,0:T(8,128)(2,1)}), bf16[8,256,512]{2,1,0:T(8,128)(2,1)}, u32[]{:S(2)}, u32[]{:S(2)}) async-start(bf16[8,256,512]{2,1,0:T(8,128)(2,1)} %bitcast.88), calls=%async_computation | async-start | bytes 4194304 | tf_op jit(solution)/shard_map/all_to_all | solution.py:108
  6.4 1.3 collective-permute-start
  7.7 2.1 %fusion.16 = bf16[2048,128]{0,1:T(8,128)(2,1)} fusion(bf16[1,2048,256]{2,1,0:T(8,128)(2,1)S(1)} %convert_element_type.77, bf16[8,256,128]{2,1,0:T(8,128)(2,1)} %constant.113.clone, s32[]{:T(128)S(6)} %select_n.92), kind=kOutput, calls=%fused_computation.30 | convolution fusion | flops 134479872 | bytes 1638404 | tf_op jit(solution)/shard_map/dot_general | solution.py:71
  9.8 3.8 %collective-permute-start.1 = (bf16[2048,128]{0,1:T(8,128)(2,1)}, bf16[2048,128]{0,1:T(8,128)(2,1)}, u32[]{:S(2)}, u32[]{:S(2)}) collective-permute-start(bf16[2048,128]{0,1:T(8,128)(2,1)} %fusion.16), channel_id=1, source_target_pairs={{0,7},{1,6},{2,5},{3,4},{4,3},{5,2},{6,1},{7,0},{8,15},{9,14},{10,... | collective-permute-start | bytes 1572872 | tf_op jit(solution)/shard_map/ppermute | solution.py:82
  14.3 0.7 constant_dynamic-slice_fusion
  15.0 2.7 %convolution_bitcast_fusion = f32[2048,256]{1,0:T(8,128)} fusion(bf16[1,2048,256]{2,1,0:T(8,128)(2,1)S(1)} %convert_element_type.77, bf16[8,256,256]{2,1,0:T(8,128)(2,1)} %constant.115.clone, s32[]{:T(128)S(6)} %select_n.92), kind=kOutput, calls=%fused_computation.14 | convolution fusion | flops 268435456 | bytes 3276804 | tf_op jit(solution)/shard_map/dot_general | solution.py:71
  17.7 1.4 convolution_bitcast_fusion.1
  19.1 12.8 %collective-permute-done = bf16[8,2048]{1,0:T(8,128)(2,1)S(1)} collective-permute-done((bf16[8,2048]{1,0:T(8,128)(2,1)S(1)}, bf16[8,2048]{1,0:T(8,128)(2,1)S(1)}, u32[]{:S(2)}, u32[]{:S(2)}) %collective-permute-start) | collective-permute-done | bytes 32800 | tf_op jit(solution)/shard_map/ppermute | solution.py:87
  31.9 2.5 %fusion.47 = f32[2048,256]{1,0:T(8,128)} fusion(bf16[8,2048]{1,0:T(8,128)(2,1)S(1)} %collective-permute-done, bf16[8,8,256]{2,1,0:T(8,128)(2,1)} %constant.117.clone, s32[]{:T(128)S(6)} %select_n.92), kind=kOutput, calls=%fused_computation.81 | convolution fusion | flops 8388608 | bytes 2134020 | tf_op jit(solution)/shard_map/dot_general | solution.py:71
  34.4 2.0 %copy.45 = bf16[8,32,8,512]{3,2,0,1:T(8,128)(2,1)S(1)} copy(bf16[8,32,8,512]{3,2,1,0:T(8,128)(2,1)} %bitcast.33) | data formatting | bytes 4194304 | tf_op jit(solution)/shard_map/all_to_all | solution.py:108
  36.7 6.4 %convolution_convert_fusion = bf16[256,2048]{1,0:T(8,128)(2,1)S(1)} fusion(bf16[2048,2048]{1,0:T(8,128)(2,1)} %constant.112.clone, bf16[256,4096]{1,0:T(8,128)(2,1)S(1)} %bitcast.89, pred[2048]{0:T(1024)(128)(4,1)S(1)} %iota_compare_fusion, s32[]{:T(128)S(6)} %select_n.91, f32[256,2048]{1,0:T(8,128)S(1)} %bitcast.97), kind=kOutput, calls=%fused_computation.28 | convolution fusion | flops 2150629376 | bytes 13633540 | tf_op jit(solution)/shard_map/dot_general | solution.py:71
  43.0 1.0 copy.53
  44.1 13.8 %all-to-all-start.1 = ((bf16[256,8,256]{2,0,1:T(8,128)(2,1)}), bf16[256,8,256]{2,0,1:T(8,128)(2,1)S(1)}, u32[]{:S(2)}, u32[]{:S(2)}) async-start(bf16[256,8,256]{2,0,1:T(8,128)(2,1)} %bitcast.82), calls=%async_computation.1 | async-start | bytes 2097152 | tf_op jit(solution)/shard_map/all_to_all | solution.py:121
  57.9 6.9 %fusion.5 = f32[2048,256]{0,1:T(8,128)} fusion(f32[2048,256]{1,0:T(8,128)} %fusion.47, f32[2048,256]{1,0:T(8,128)} %convolution_bitcast_fusion, bf16[2048,128]{0,1:T(8,128)(2,1)} %collective-permute-done.1, bf16[8,128,256]{2,1,0:T(8,128)(2,1)} %constant.116.clone, s32[]{:T(128)S(6)} %select_n.92), kind=kOutput, calls=%fused_computation.8 | convolution fusion | flops 2337800192 | bytes 6881284 | tf_op jit(solution)/shard_map/dot_general | solution.py:71
  64.8 3.4 %fusion.11 = f32[2048,256]{0,1:T(8,128)} fusion(f32[2048,256]{0,1:T(8,128)} %fusion.5, f32[2048,256]{0,1:T(8,128)S(1)} %convolution_bitcast_fusion.1, bf16[8,2048]{1,0:T(8,128)(2,1)S(1)} %collective-permute-done, f32[256]{0:T(256)S(1)} %bitcast.96, bf16[8,8,256]{2,1,0:T(8,128)(2,1)} %constant.118.clone, s32[]{:T(128)S(6)} %select_n.92), kind=kOutput, calls=%fused_computation.19 | convolution fusion | flops 9961472 | bytes 6329348 | tf_op jit(solution)/shard_map/dot_general | solution.py:71
  68.3 1.6 all-to-all-done.1
  69.9 12.5 %fusion.31 = f32[4096,256]{0,1:T(8,128)} fusion(bf16[4096,2048]{1,0:T(8,128)(2,1)} %constant.128, bf16[256,8,256]{2,0,1:T(8,128)(2,1)S(1)} %all-to-all-done.1), kind=kOutput, calls=%fused_computation.55 | convolution fusion | flops 4294967296 | bytes 22020096 | tf_op jit(solution)/shard_map/dot_general | solution.py:71
  82.3 3.1 %add_select_fusion.1 = (f32[2048,128]{0,1:T(8,128)S(1)}, f32[2048,128]{0,1:T(8,128)S(1)}, f32[2048,128]{0,1:T(8,128)S(1)}, f32[2048,128]{0,1:T(8,128)S(1)}) fusion(f32[4096,256]{0,1:T(8,128)} %fusion.31, pred[128]{0:T(512)(128)(4,1)S(1)} %compare_and_fusion.2), kind=kLoop, calls=%fused_computation.40 | loop fusion | flops 1835008 | bytes 8388736 | tf_op jit(solution)/shard_map/jit(_where)/select_n | solution.py:128
  85.5 6.0 %fusion.29 = f32[256,2048]{1,0:T(8,128)S(1)} fusion(bf16[2048,2048]{1,0:T(8,128)(2,1)} %constant.129, f32[2048,256]{0,1:T(8,128)S(1)} %copy-done, f32[2048,128]{0,1:T(8,128)S(1)} %get-tuple-element.8, f32[2048,128]{0,1:T(8,128)S(1)} %get-tuple-element.10), kind=kOutput, calls=%fused_computation.54 | convolution fusion | flops 2149056512 | bytes 14680064 | tf_op jit(solution)/shard_map/dot_general | solution.py:71
  91.5 2.5 %fusion.13 = bf16[256,2048]{1,0:T(8,128)(2,1)S(1)} fusion(f32[256,2048]{1,0:T(8,128)S(1)} %fusion.29, bf16[2048,2048]{1,0:T(8,128)(2,1)S(1)} %bitcast.102, f32[2048,256]{0,1:T(8,128)S(1)} %copy-done, f32[2048,128]{0,1:T(8,128)S(1)} %get-tuple-element.9, f32[2048,128]{0,1:T(8,128)S(1)} %get-tuple-element.7), kind=kOutput, calls=%fused_computation.25 | convolution fusion | flops 2150105088 | bytes 15728640 | tf_op jit(solution)/shard_map/dot_general | solution.py:71
  94.1 20.0 %all_to_all.70 = bf16[8,256,256]{1,2,0:T(8,128)(2,1)S(1)} all-to-all(bf16[8,256,256]{1,2,0:T(8,128)(2,1)S(1)} %bitcast.87), channel_id=1, replica_groups=mesh['ptg'=4,'img'=8] {'img'}, dimensions={0} | all-to-all | bytes 2097152 | tf_op jit(solution)/shard_map/all_to_all | solution.py:131
  114.1 3.5 %fusion.14 = bf16[256,2048]{1,0:T(8,128)(2,1)S(1)} fusion(bf16[256,2048]{0,1:T(8,128)(2,1)S(1)} %bitcast.91, bf16[2048,2048]{1,0:T(8,128)(2,1)S(1)} %bitcast.100, s32[]{:T(128)S(6)} %select_n.91, f32[256,2048]{1,0:T(8,128)S(1)} %bitcast.98), kind=kOutput, calls=%fused_computation.26 | convolution fusion | flops 2149056512 | bytes 12582916 | tf_op jit(solution)/shard_map/dot_general | solution.py:71
  117.7 1.1 copy.51
  118.7 5.3 %all-to-all-start.3 = ((bf16[256,4,512]{2,0,1:T(8,128)(2,1)}), bf16[256,4,512]{2,0,1:T(8,128)(2,1)S(1)}, u32[]{:S(2)}, u32[]{:S(2)}) async-start(bf16[256,4,512]{2,0,1:T(8,128)(2,1)} %bitcast.80), calls=%async_computation.3 | async-start | bytes 2097152 | tf_op jit(solution)/shard_map/all_to_all | solution.py:133
  124.0 0.6 dynamic-slice
  124.6 0.7 dynamic-update-slice
  125.3 24.1 %all-reduce = s32[4]{0:T(128)S(1)} all-reduce(s32[4]{0:T(128)S(1)} %dynamic-update-slice), channel_id=1, replica_groups=mesh['ptg'=4,'img'=8] {'ptg'}, use_global_device_ids=true, to_apply=%add | all-reduce | flops 4 | bytes 32
  150.1 3.5 %collective-permute-start.2 = (bf16[256,512]{1,0:T(8,128)(2,1)S(1)}, bf16[256,512]{1,0:T(8,128)(2,1)S(1)}, u32[]{:S(2)}, u32[]{:S(2)}) collective-permute-start(bf16[256,512]{1,0:T(8,128)(2,1)S(1)} %get-tuple-element.12), channel_id=1, source_target_pairs={{0,0},{1,4},{2,8},{3,12},{4,16},{5,20},{6,24},{7,28},{8,1},{9,5},{... | collective-permute-start | bytes 786440 | tf_op jit(solution)/shard_map/ppermute | solution.py:158
  155.6 0.7 dynamic_slice.50
  158.8 24.2 %collective-permute-done.2 = bf16[256,512]{1,0:T(8,128)(2,1)S(1)} collective-permute-done((bf16[256,512]{1,0:T(8,128)(2,1)S(1)}, bf16[256,512]{1,0:T(8,128)(2,1)S(1)}, u32[]{:S(2)}, u32[]{:S(2)}) %collective-permute-start.2) | collective-permute-done | bytes 262176 | tf_op jit(solution)/shard_map/ppermute | solution.py:158
  183.2 4.4 %collective-permute-done.3 = bf16[256,512]{1,0:T(8,128)(2,1)S(1)} collective-permute-done((bf16[256,512]{1,0:T(8,128)(2,1)S(1)}, bf16[256,512]{1,0:T(8,128)(2,1)S(1)}, u32[]{:S(2)}, u32[]{:S(2)}) %collective-permute-start.3) | collective-permute-done | bytes 262176 | tf_op jit(solution)/shard_map/ppermute | solution.py:158
  187.6 0.9 convert_dynamic-update-slice_fusion
  (46 shorter events, 2.9 us)
Async XLA Ops:
  0.0 5.4 %copy-start.1 = (s32[1,2048,256]{2,1,0:T(8,128)S(1)}, s32[1,2048,256]{2,1,0:T(8,128)}, u32[]{:S(2)}) copy-start(s32[1,2048,256]{2,1,0:T(8,128)} %param.18) | copy-start | bytes 6291460
  0.0 34.4 %all-to-all-start = ((bf16[8,256,512]{2,1,0:T(8,128)(2,1)}), bf16[8,256,512]{2,1,0:T(8,128)(2,1)}, u32[]{:S(2)}, u32[]{:S(2)}) async-start(bf16[8,256,512]{2,1,0:T(8,128)(2,1)} %bitcast.88), calls=%async_computation | async-start | bytes 4194304 | tf_op jit(solution)/shard_map/all_to_all | solution.py:108
  5.4 0.7 copy-start.3
  6.4 25.5 %collective-permute-start = (bf16[8,2048]{1,0:T(8,128)(2,1)S(1)}, bf16[8,2048]{1,0:T(8,128)(2,1)S(1)}, u32[]{:S(2)}, u32[]{:S(2)}) collective-permute-start(bf16[8,2048]{1,0:T(8,128)(2,1)S(1)} %convolution_convert_fusion.2), channel_id=1, source_target_pairs={{4,0},{7,1},{6,2},{5,3},{12,8},{15,9},{14,10},{13,11},{20,16},{23,... | collective-permute-start | bytes 98312 | tf_op jit(solution)/shard_map/ppermute | solution.py:87
  9.8 48.1 %collective-permute-start.1 = (bf16[2048,128]{0,1:T(8,128)(2,1)}, bf16[2048,128]{0,1:T(8,128)(2,1)}, u32[]{:S(2)}, u32[]{:S(2)}) collective-permute-start(bf16[2048,128]{0,1:T(8,128)(2,1)} %fusion.16), channel_id=1, source_target_pairs={{0,7},{1,6},{2,5},{3,4},{4,3},{5,2},{6,1},{7,0},{8,15},{9,14},{10,... | collective-permute-start | bytes 1572872 | tf_op jit(solution)/shard_map/ppermute | solution.py:82
  34.4 2.2 %copy-start.4 = (f32[1,256,2048]{2,1,0:T(8,128)S(1)}, f32[1,256,2048]{2,1,0:T(8,128)}, u32[]{:S(2)}) copy-start(f32[1,256,2048]{2,1,0:T(8,128)} %param.17) | copy-start | bytes 6291460
  44.1 25.8 %all-to-all-start.1 = ((bf16[256,8,256]{2,0,1:T(8,128)(2,1)}), bf16[256,8,256]{2,0,1:T(8,128)(2,1)S(1)}, u32[]{:S(2)}, u32[]{:S(2)}) async-start(bf16[256,8,256]{2,0,1:T(8,128)(2,1)} %bitcast.82), calls=%async_computation.1 | async-start | bytes 2097152 | tf_op jit(solution)/shard_map/all_to_all | solution.py:121
  82.3 3.1 %copy-start = (f32[2048,256]{0,1:T(8,128)S(1)}, f32[2048,256]{0,1:T(8,128)}, u32[]{:S(2)}) copy-start(f32[2048,256]{0,1:T(8,128)} %fusion.11) | copy-start | bytes 6291460
  82.3 9.1 %slice-start.2 = ((s8[8388608]{0:T(1024)(128)(4,1)}), s8[4194304]{0:T(1024)(128)(4,1)S(1)}, s32[]{:S(2)}) async-start(s8[8388608]{0:T(1024)(128)(4,1)} %bitcast.101), calls=%async_computation.6 | async-start | bytes 8388608
  85.5 6.0 %slice-start.3 = ((s8[8388608]{0:T(1024)(128)(4,1)}), s8[4194304]{0:T(1024)(128)(4,1)S(1)}, s32[]{:S(2)}) async-start(s8[8388608]{0:T(1024)(128)(4,1)} %bitcast.101), calls=%async_computation.7 | async-start | bytes 8388608
  85.5 28.6 %slice-start = ((s8[8388608]{0:T(1024)(128)(4,1)}), s8[4194304]{0:T(1024)(128)(4,1)S(1)}, s32[]{:S(2)}) async-start(s8[8388608]{0:T(1024)(128)(4,1)} %bitcast.99), calls=%async_computation.4 | async-start | bytes 8388608
  91.5 22.6 %slice-start.1 = ((s8[8388608]{0:T(1024)(128)(4,1)}), s8[4194304]{0:T(1024)(128)(4,1)S(1)}, s32[]{:S(2)}) async-start(s8[8388608]{0:T(1024)(128)(4,1)} %bitcast.99), calls=%async_computation.5 | async-start | bytes 8388608
  94.0 20.1 %copy-start.5 = (f32[1,256,2048]{2,1,0:T(8,128)S(1)}, f32[1,256,2048]{2,1,0:T(8,128)}, u32[]{:S(2)}) copy-start(f32[1,256,2048]{2,1,0:T(8,128)} %param.17) | copy-start | bytes 6291460
  117.6 6.4 %copy-start.8 = (u32[32]{0:T(128)S(1)}, u32[32]{0:T(128)}, u32[]{:S(2)}) copy-start(u32[32]{0:T(128)} %constant.133) | copy-start | bytes 388
  118.7 35.0 %copy-start.7 = (s32[32]{0:T(128)S(1)}, s32[32]{0:T(128)}, u32[]{:S(2)}) copy-start(s32[32]{0:T(128)} %constant.121.clone) | copy-start | bytes 388
  118.7 36.9 %copy-start.6 = (s32[32]{0:T(128)S(1)}, s32[32]{0:T(128)}, u32[]{:S(2)}) copy-start(s32[32]{0:T(128)} %constant.122.clone) | copy-start | bytes 388
  118.7 30.8 %all-to-all-start.3 = ((bf16[256,4,512]{2,0,1:T(8,128)(2,1)}), bf16[256,4,512]{2,0,1:T(8,128)(2,1)S(1)}, u32[]{:S(2)}, u32[]{:S(2)}) async-start(bf16[256,4,512]{2,0,1:T(8,128)(2,1)} %bitcast.80), calls=%async_computation.3 | async-start | bytes 2097152 | tf_op jit(solution)/shard_map/all_to_all | solution.py:133
  150.1 32.9 %collective-permute-start.2 = (bf16[256,512]{1,0:T(8,128)(2,1)S(1)}, bf16[256,512]{1,0:T(8,128)(2,1)S(1)}, u32[]{:S(2)}, u32[]{:S(2)}) collective-permute-start(bf16[256,512]{1,0:T(8,128)(2,1)S(1)} %get-tuple-element.12), channel_id=1, source_target_pairs={{0,0},{1,4},{2,8},{3,12},{4,16},{5,20},{6,24},{7,28},{8,1},{9,5},{... | collective-permute-start | bytes 786440 | tf_op jit(solution)/shard_map/ppermute | solution.py:158
  153.6 33.9 %collective-permute-start.3 = (bf16[256,512]{1,0:T(8,128)(2,1)S(1)}, bf16[256,512]{1,0:T(8,128)(2,1)S(1)}, u32[]{:S(2)}, u32[]{:S(2)}) collective-permute-start(bf16[256,512]{1,0:T(8,128)(2,1)S(1)} %get-tuple-element.11), channel_id=1, source_target_pairs={{0,4},{1,0},{2,12},{3,8},{4,20},{5,16},{6,28},{7,24},{8,5},{9,1},{... | collective-permute-start | bytes 786440 | tf_op jit(solution)/shard_map/ppermute | solution.py:158
  183.2 4.4 %copy-start.2 = (f32[512,512]{1,0:T(8,128)}, f32[512,512]{1,0:T(8,128)S(1)}, u32[]{:S(2)}) copy-start(f32[512,512]{1,0:T(8,128)S(1)} %convert_dynamic-update-slice_fusion.1) | copy-start | bytes 3145732

commit v2 on v0

v2 whole, which is shorter than its diff:
```python
import jax
import jax.numpy as jnp
import numpy as np
from jax import lax
from jax.experimental import pallas as pl
from jax.experimental.pallas import tpu as pltpu
from jax.sharding import PartitionSpec as P


def make_tables(points):
    angle = 2.0 * np.pi / points * np.arange(points)
    cos_of, sin_of = np.cos(angle), -np.sin(angle)
    index = np.arange(points, dtype=np.int64)
    coarse = index[::8, None] * index[None, :] % points
    fine = index[:8, None] * index[None, :] % points
    return [t[p].astype(np.float32) for p in (coarse, fine) for t in (cos_of, sin_of)]


MESH = pl.DeviceIdType.MESH
BLOCK = 256


def dot(a, b, dims=((1,), (0,))):
    return lax.dot_general(a, b, (dims, ((), ())), preferred_element_type=jnp.float32)


def remote(src, dst, send, recv, device):
    return pltpu.make_async_remote_copy(
        src_ref=src, dst_ref=dst, send_sem=send, recv_sem=recv, device_id=device, device_id_type=MESH
    )


def arrived(ref, sem):
    pltpu.make_async_copy(ref, ref, sem).wait()


def kernel(
    image, beam_hbm, counts_hbm, start, coarse_cos_hbm, coarse_sin_hbm, fine_cos, fine_sin,
    sums,
    column, coarse_cos, coarse_sin, beam, counts, strip, beamed, row_out, col_in, weighted, back_out, back_in,
    real_in, imag_in, given, terms, starts, values, weight, sent, recv, mirror, first_out, first_in,
    load_sem, own_sem, image_send, image_recv, row_send, row_recv, back_send, back_recv,
    layer_send, layer_recv, start_send, start_recv, count_sem,
):
    parts, rows, tile = strip.shape
    layers, _, chunk = terms.shape
    folds = sums.shape[0]
    points = rows * parts
    wide = counts.shape[1]
    half = wide // 2
    me, layer = lax.axis_index("img"), lax.axis_index("ptg")

    def peer(k):
        return lax.rem(me + k, parts)

    def above(k):
        return lax.rem(layer + k, layers)

    def rows_of(d):
        return pl.ds(pl.multiple_of(d * rows, rows), rows)

    loads = [
        pltpu.make_async_copy(src, dst, load_sem.at[at])
        for at, (src, dst) in enumerate(
            [(counts_hbm, counts), (coarse_cos_hbm, coarse_cos), (coarse_sin_hbm, coarse_sin), (beam_hbm, beam)]
        )
    ]
    mine = pltpu.make_async_copy(image.at[rows_of(me), :], strip.at[me], own_sem)
    mine.start()
    for load in loads:
        load.start()

    barrier = pltpu.get_barrier_semaphore()
    for k in range(1, parts):
        pl.semaphore_signal(barrier, inc=1, device_id=(layer, peer(k)), device_id_type=MESH)
    for k in range(1, layers):
        pl.semaphore_signal(barrier, inc=1, device_id=(above(k), me), device_id_type=MESH)
    pl.semaphore_wait(barrier, parts + layers - 2)

    def image_copy(k):
        d = peer(k)
        return remote(image.at[rows_of(d), :], strip.at[me], image_send.at[k], image_recv.at[me], (layer, d))

    def start_copy(k):
        return remote(start, starts.at[layer], start_send.at[k], start_recv.at[layer], (above(k), me))

    for k in range(1, parts):
        image_copy(k).start()
    for k in range(1, layers):
        start_copy(k).start()
    starts[layer] = start[...]

    low = me < parts // 2

    def grid(shape):
        return lax.broadcasted_iota(jnp.int32, shape, 0), lax.broadcasted_iota(jnp.int32, shape, 1)

    def ones(where):
        return jnp.where(where, 1.0, 0.0).astype(jnp.bfloat16)

    def at_low(where):
        return jnp.logical_and(where, low)

    def at_high(where):
        return jnp.logical_and(where, jnp.logical_not(low))

    def at_first(where):
        return jnp.logical_and(where, me == 0)

    loads[0].wait()
    values[...] = counts[...].astype(jnp.float32).astype(jnp.bfloat16)
    i, j = grid((wide, sent.shape[1]))
    sel = at_low((i == half + j) & (j < half)) | at_high((i == wide - j) & (j >= 1) & (j < half))
    sent[...] = dot(values[...], ones(sel)).astype(jnp.bfloat16)
    i, j = grid((16, wide))
    first_out[...] = dot(ones(i + j == 0), values[...], ((1,), (1,))).astype(jnp.bfloat16)
    other = lax.rem(parts - me, parts)
    other = jnp.where(me == 0, parts // 2, jnp.where(me == parts // 2, 0, other))
    count_copy = remote(sent, recv, count_sem.at[0], count_sem.at[1], (layer, parts - 1 - me))
    first_copy = remote(first_out, first_in, count_sem.at[2], count_sem.at[3], (layer, other))
    count_copy.start()
    first_copy.start()

    loads[1].wait()
    loads[2].wait()

    @pl.loop(0, points // 64)
    def _(g):
        eight = pl.ds(pl.multiple_of(g * 8, 8), 8)
        for c in range(0, points, 256):
            at = pl.ds(c, 256)
            cos_a, sin_a = coarse_cos[eight, at], coarse_sin[eight, at]
            cos_b, sin_b = fine_cos[:, at], fine_sin[:, at]
            for r in range(0, 8, 2):
                cos_rows, sin_rows = [], []
                for t in (r, r + 1):
                    cos_t, sin_t = cos_a[t : t + 1], sin_a[t : t + 1]
                    cos_rows.append(cos_t * cos_b - sin_t * sin_b)
                    sin_rows.append(sin_t * cos_b + cos_t * sin_b)
                to = pl.multiple_of(g * 64 + r * 8, 16)
                column[pl.ds(to, 16), at] = jnp.concatenate(cos_rows, 0).astype(jnp.bfloat16)
                column[pl.ds(points + to, 16), at] = jnp.concatenate(sin_rows, 0).astype(jnp.bfloat16)

    loads[3].wait()
    mine.wait()
    origin = start[0:1, 0:1]
    per_fold = points // tile
    for t in range(per_fold):
        for f in range(folds):
            src = t + per_fold * f

            @pl.when(src != me)
            def _():
                arrived(strip.at[src], image_recv.at[src])

        place = lax.broadcasted_iota(jnp.int32, (rows, tile), 1) + t * tile
        window = strip[t + per_fold * (folds - 1)].astype(jnp.float32)
        for f in range(folds - 2, -1, -1):
            window = jnp.where(place + f * points >= origin, strip[t + per_fold * f].astype(jnp.float32), window)
        at = pl.ds(t * tile, tile)
        beamed[:, at] = (beam[:, at] * window).astype(jnp.bfloat16)

    def columns_of(d):
        return pl.ds(pl.multiple_of(d * wide, wide), wide)

    def row_copy(d):
        return remote(row_out.at[d], col_in.at[rows_of(me), :], row_send.at[d], row_recv.at[me], (layer, d))

    _, j = grid((rows, points))
    sides = jnp.where(lax.rem(j, 2) == 0, beamed[...].astype(jnp.float32), -beamed[...].astype(jnp.float32))
    alternating = jnp.sum(sides, 1, keepdims=True)
    _, lane = grid((rows, wide))

    @pl.loop(0, parts // 2)
    def _(step):
        d = lax.rem(me + 1 + step, parts // 2)
        real = dot(beamed[...], column[:points, columns_of(d)])
        imag = dot(beamed[...], column[points:, columns_of(d)])
        imag = jnp.where(jnp.logical_and(lane == 0, d == 0), alternating, imag)
        lower = jnp.where(lane < half, real, pltpu.roll(imag, half, 1)).astype(jnp.bfloat16)
        upper = jnp.where(lane < half, pltpu.roll(real, half, 1), imag).astype(jnp.bfloat16)
        for to, block in ((d, lower), (parts - 1 - d, upper)):

            @pl.when(to == me)
            def _():
                col_in[rows_of(me), :] = block

            @pl.when(to != me)
            def _():
                row_out[to] = block
                row_copy(to).start()

    count_copy.wait()
    first_copy.wait()
    steps = points // BLOCK

    def block_of(b):
        return pl.ds(pl.multiple_of(b * BLOCK, BLOCK), BLOCK)

    i, j = grid((wide, wide))
    own = jnp.logical_and(
        at_low(i == lax.rem(j, half)) | at_high(i == half - lax.rem(j, half)),
        jnp.logical_not(at_first(j == half)),
    )
    own_a, own_b = ones(at_low(own)), ones(at_high(own) | at_first(i + j == 0))
    i, j = grid((recv.shape[1], wide))
    expand = i == lax.rem(j, half)
    recv_a, recv_b = ones(at_high(expand)), ones(at_low(expand))
    i, j = grid((16, wide))
    packed = at_first((i == 0) & (j == half))
    first_a, first_b = ones(packed), ones(packed | at_low((i == 0) & (lax.rem(j, half) == 0) & (me != 0)))
    i, j = grid((BLOCK, BLOCK))
    flip, flip_first = ones(i + j == BLOCK), ones(i + j == 0)
    _, j = grid((1, wide))
    packed = at_first(lax.rem(j, half) == 0)
    scale_row = jnp.where(packed, 0.5, 1.0) * (1.0 / float(points * points))
    sign = jnp.where(packed, 0.0, jnp.where(j < half, -1.0, 1.0))

    mirror[...] = dot(first_in[...], first_b, ((0,), (0,))).astype(jnp.bfloat16)
    weight[...] = dot(first_in[...], first_a, ((0,), (0,))).astype(jnp.bfloat16)

    @pl.loop(0, steps)
    def _(b):
        at = block_of(b)
        total = dot(recv[at, :], recv_b) + dot(values[at, :], own_b)
        mirror[at, :] = (mirror[at, :].astype(jnp.float32) + total).astype(jnp.bfloat16)

    @pl.loop(0, steps)
    def _(b):
        at = block_of(b)
        total = dot(flip, mirror[block_of(steps - 1 - b), :])
        total += dot(flip_first, mirror[block_of(lax.rem(steps - b, steps)), :])
        total += dot(values[at, :], own_a) + dot(recv[at, :], recv_a)
        weight[at, :] = ((weight[at, :].astype(jnp.float32) + total) * scale_row).astype(jnp.bfloat16)

    for k in range(1, parts):
        src = lax.rem(me + parts - k, parts)
        arrived(col_in.at[rows_of(src), :], row_recv.at[src])

    @pl.loop(0, steps)
    def _(b):
        at = block_of(b)
        low = block_of(b + steps)
        cos_part = dot(column[at, :], col_in[...])
        sin_part = dot(column[low, :], col_in[...])
        scale = weight[at, :].astype(jnp.float32)
        weighted[at, :] = (scale * (cos_part + sign * pltpu.roll(sin_part, half, 1))).astype(jnp.bfloat16)
        weighted[low, :] = (scale * (sin_part - sign * pltpu.roll(cos_part, half, 1))).astype(jnp.bfloat16)

    def inverse(d):
        upper = dot(column[rows_of(d), :], weighted[:points, :])
        lower = dot(column[rows_of(d + parts), :], weighted[points:, :])
        return (upper + lower).astype(jnp.bfloat16)

    def back_copy(k):
        d = peer(k)
        return remote(back_out.at[d], back_in.at[me], back_send.at[k], back_recv.at[me], (layer, d))

    @pl.loop(1, parts)
    def _(k):
        d = peer(k)
        back_out[d] = inverse(d)
        back_copy(k).start()

    back_in[me] = inverse(me)
    for k in range(1, parts):
        src = lax.rem(me + parts - k, parts)
        arrived(back_in.at[src], back_recv.at[src])
    for d in range(parts // 2):
        lower = back_in[d].astype(jnp.float32)
        upper = back_in[parts - 1 - d].astype(jnp.float32)
        at = pl.ds(d * wide, wide)
        real_in[:, at] = jnp.where(lane < half, lower, pltpu.roll(upper, half, 1)).astype(jnp.bfloat16)
        imag_in[:, at] = jnp.where(lane < half, pltpu.roll(lower, half, 1), upper).astype(jnp.bfloat16)

    def chunk_of(q):
        return pl.ds(pl.multiple_of(q * chunk, chunk), chunk)

    def contribution(q):
        pixels = dot(real_in[...], column[: points // 2, chunk_of(q)])
        pixels += dot(imag_in[...], column[points : points + points // 2, chunk_of(q)])
        middle = imag_in[:, 0:1].astype(jnp.float32)
        _, at = grid((rows, chunk))
        pixels += jnp.where(lax.rem(at, 2) == 0, middle, -middle)
        return (beam[:, chunk_of(q)] * pixels).astype(jnp.bfloat16)

    def layer_copy(k):
        q = above(k)
        return remote(given.at[q], terms.at[layer], layer_send.at[k], layer_recv.at[layer], (q, me))

    @pl.loop(1, layers)
    def _(k):
        q = above(k)
        given[q] = contribution(q)
        layer_copy(k).start()

    terms[layer] = contribution(layer)
    for k in range(1, layers):
        src = lax.rem(layer + layers - k, layers)
        arrived(starts.at[src], start_recv.at[src])
        arrived(terms.at[src], layer_recv.at[src])

    place = lax.broadcasted_iota(jnp.int32, (rows, chunk), 1) + layer * chunk
    for f in range(folds):
        total = jnp.zeros((rows, chunk), jnp.float32)
        for p in range(layers):
            offset = place + f * points - starts[p][0:1, 0:1]
            inside = (offset >= 0) & (offset < points)
            total += jnp.where(inside, terms[p].astype(jnp.float32), 0.0)
        sums[f] = total.astype(jnp.bfloat16)

    for k in range(1, parts):
        image_copy(k).wait_send()
        back_copy(k).wait_send()
        row_copy(peer(k)).wait_send()
    for k in range(1, layers):
        start_copy(k).wait_send()
        layer_copy(k).wait_send()


def strips(image, beam, counts, start, layers):
    points, wide = counts.shape
    rows, tile = beam.shape[0], image.shape[1]
    parts = points // rows
    folds = tile * parts // points
    chunk = points // layers
    coarse_cos, coarse_sin, fine_cos, fine_sin = (jnp.asarray(t) for t in make_tables(points))
    hp = max(wide // 2, 128)
    vmem, hbm = pl.BlockSpec(memory_space=pltpu.VMEM), pl.BlockSpec(memory_space=pl.ANY)
    bf = jnp.bfloat16
    dma = pltpu.SemaphoreType.DMA
    return pl.pallas_call(
        kernel,
        out_shape=jax.ShapeDtypeStruct((folds, rows, chunk), bf),
        in_specs=[hbm, hbm, hbm, vmem, hbm, hbm, vmem, vmem],
        out_specs=vmem,
        scratch_shapes=[
            pltpu.VMEM((2 * points, points), bf),
            pltpu.VMEM((points // 8, points), jnp.float32),
            pltpu.VMEM((points // 8, points), jnp.float32),
            pltpu.VMEM((rows, points), jnp.float32),
            pltpu.VMEM((points, wide), jnp.int32),
            pltpu.VMEM((parts, rows, tile), bf),
            pltpu.VMEM((rows, points), bf),
            pltpu.VMEM((parts, rows, wide), bf),
            pltpu.VMEM((points, wide), bf),
            pltpu.VMEM((2 * points, wide), bf),
            pltpu.VMEM((parts, rows, wide), bf),
            pltpu.VMEM((parts, rows, wide), bf),
            pltpu.VMEM((rows, points // 2), bf),
            pltpu.VMEM((rows, points // 2), bf),
            pltpu.VMEM((layers, rows, chunk), bf),
            pltpu.VMEM((layers, rows, chunk), bf),
            pltpu.VMEM((layers, 8, 128), jnp.int32),
            pltpu.VMEM((points, wide), bf),
            pltpu.VMEM((points, wide), bf),
            pltpu.VMEM((points, hp), bf),
            pltpu.VMEM((points, hp), bf),
            pltpu.VMEM((points, wide), bf),
            pltpu.VMEM((16, points), bf),
            pltpu.VMEM((16, points), bf),
            dma((4,)), dma(()), dma((parts,)), dma((parts,)), dma((parts,)), dma((parts,)),
            dma((parts,)), dma((parts,)), dma((layers,)), dma((layers,)), dma((layers,)), dma((layers,)),
            dma((4,)),
        ],
        compiler_params=pltpu.CompilerParams(
            collective_id=0, has_side_effects=True, vmem_limit_bytes=60 * 1024 * 1024
        ),
    )(image, beam, counts, start, coarse_cos, coarse_sin, fine_cos, fine_sin)


def shards(image, beam, counts, offsets):
    points = counts.shape[1]
    parts, layers = lax.axis_size("img"), lax.axis_size("ptg")
    me, layer = lax.axis_index("img"), lax.axis_index("ptg")
    tile = image.shape[1]
    folds = tile * parts // points
    rows = points // parts
    chunk = points // layers
    start = offsets[0]
    twice = jnp.concatenate([beam[0], beam[0]], 1)
    rolled = lax.dynamic_slice_in_dim(twice, points - start % points, points, 1)
    sums = strips(image, rolled, counts[0], jnp.full((8, 128), start, jnp.int32), layers)

    out_rows = points // layers
    tall, broad = out_rows // rows, tile // chunk
    out = jnp.zeros((out_rows, tile), jnp.float32)
    for s in range(folds):
        pairs = []
        row_at = np.zeros((layers * parts,), np.int32)
        col_at = np.zeros((layers * parts,), np.int32)
        for p in range(layers):
            for i in range(parts):
                f = (i % tall * broad + p % broad + s) % folds
                q, c = i * rows // out_rows, (points * f + chunk * p) // tile
                pairs.append((p * parts + i, q * parts + c))
                row_at[q * parts + c] = i * rows - q * out_rows
                col_at[q * parts + c] = points * f + chunk * p - tile * c
        piece = lax.dynamic_index_in_dim(sums, (me % tall * broad + layer % broad + s) % folds, 0, False)
        piece = lax.ppermute(piece, ("ptg", "img"), pairs)
        here = layer * parts + me
        out = lax.dynamic_update_slice(
            out, piece.astype(jnp.float32), (jnp.asarray(row_at)[here], jnp.asarray(col_at)[here])
        )
    return out


def solution(mesh):
    return jax.shard_map(
        shards,
        mesh=mesh,
        in_specs=(P(None, "img"), P("ptg", "img", None), P("ptg", None, "img"), P("ptg")),
        out_specs=P("ptg", "img"),
        check_vma=False,
    )
```

time: 1030 us -> 144 us (0.14)
  matrix products: 829 us -> 0 us
  Pallas kernels: 0 us -> 95.5 us
  waiting for transfers between devices: 109 us -> 33 us
  blocking collectives: 29.4 us -> 0 us
  starting transfers between devices: 25.8 us -> 2.79 us
  local copies, waits for them, and re-layouts: 16.2 us -> 2.96 us
    dot_general x12 -> x0, matrix products: 829 us -> none  [the longest x1 72.7 us: shards(): jnp.dot(sine_table, weighted_real, preferred_element_type=jnp.float32)]
    pallas_call x0 -> x1, Pallas kernels: none -> 95.5 us  [strips(): pl.pallas_call(kernel, out_shape=jax.ShapeDtypeStruct((folds, rows, chunk...]
    psum x1 -> x0, waiting for transfers between devices: 86.3 us -> none  [shards(): lax.psum(tile_terms.astype(jnp.bfloat16), 'ptg').astype(jnp.float32)]
    ppermute x0 -> x2, waiting for transfers between devices: none -> 33 us  [shards(): piece = lax.ppermute(piece, ('ptg', 'img'), pairs)]
    all_to_all x1 -> x0, blocking collectives: 29.4 us -> none  [shards(): lax.all_to_all(placed, 'img', split_axis=1, concat_axis=0, tiled=True)]
    all_to_all x5 -> x0, starting transfers between devices: 25.3 us -> none  [the longest x1 7.16 us: shards(): lax.all_to_all(row_real, 'img', split_axis=1, concat_axis=0, tiled=True)]
    all_to_all x5 -> x0, waiting for transfers between devices: 22.5 us -> none  [the longest x1 22.5 us: shards(): lax.all_to_all(image, 'img', split_axis=0, concat_axis=1, tiled=True)]
  transfers between devices with their start and end apart: 6 -> 2, of which waited for: 2 -> 2; matrix products, arithmetic and copies ran while one was open for 27% -> 1% of each run, Pallas kernels for 0% -> 0%
where the time goes in v2:
time: 144 us
  Pallas kernels  95.5 us (66%)
  waiting for transfers between devices  33 us (23%)
  other arithmetic  5.01 us (3%)
  between operations  4.39 us (3%)
  local copies, waits for them, and re-layouts  2.96 us (2%)
  starting transfers between devices  2.79 us (2%)
    pallas_call x1, Pallas kernels, strips(): pl.pallas_call(kernel, out_shape=jax.ShapeDtypeStruct((folds, rows, chunk...  95.5 us
    ppermute x2, waiting for transfers between devices, shards(): piece = lax.ppermute(piece, ('ptg', 'img'), pairs)  33 us
    concatenate x1, other arithmetic, shards(): twice = jnp.concatenate([beam[0], beam[0]], 1)  4.09 us
  transfers between devices with their start and end apart: 2, of which 2 were waited for; matrix products, arithmetic and copies ran while one was open for 1% of the time, Pallas kernels for 0%

profile of v2, /device:TPU:1, one launch (start us, length us, event | category | flops | bytes accessed | tf_op | source)
XLA Modules:
  0.0 143.6 jit_solution(15865939676452543069)
XLA Ops:
  0.7 4.1 %fusion.beam_hbm = f32[256,2048]{1,0:T(8,128)} fusion(s32[]{:T(128)S(6)} %select_n.50, f32[256,2048]{1,0:T(8,128)} %bitcast.14), kind=kLoop, calls=%fused_computation.2 | loop fusion | flops 524288 | bytes 4194308 | tf_op jit(solution)/shard_map/concatenate | solution.py:381
  4.8 0.6 broadcast_in_dim.7.start
  5.4 0.0 copy-start.2
  5.4 0.0 copy-start.1
  5.4 95.5 %shard_map.110 = bf16[2,256,512]{2,1,0:T(8,128)(2,1)} custom-call(bf16[2048,512]{1,0:T(8,128)(2,1)} %image.1, f32[256,2048]{1,0:T(8,128)} %fusion.beam_hbm, s32[2048,256]{1,0:T(8,128)} %bitcast.13, s32[8,128]{1,0:T(8,128)} %broadcast_in_dim.7.start, f32[256,2048]{1,0:T(8,128)} %constant.86.clone.coarse_cos_hbm, f32[256,2048]{1,0:T(8,128)} %constant.87.clone.coarse_sin_hbm, ...), custom_call_target="tpu_custom_call" | custom-call | tf_op jit(solution)/shard_map/pallas_call | solution.py:332
  100.8 1.1 dynamic-slice_bitcast_fusion
  101.9 2.7 %collective-permute-start = (bf16[256,512]{1,0:T(8,128)(2,1)S(1)}, bf16[256,512]{1,0:T(8,128)(2,1)S(1)}, u32[]{:S(2)}, u32[]{:S(2)}) collective-permute-start(bf16[256,512]{1,0:T(8,128)(2,1)S(1)} %get-tuple-element.6), channel_id=1, source_target_pairs={{0,0},{1,4},{2,8},{3,12},{4,16},{5,20},{6,24},{7,28},{8,1},{9,5},{... | collective-permute-start | bytes 786440 | tf_op jit(solution)/shard_map/ppermute | solution.py:400
  104.6 0.1 collective-permute-start.1
  104.7 0.0 copy-done.2
  104.7 0.6 dynamic_slice.20
  106.6 0.0 copy-done.1
  106.6 0.6 dynamic_slice.22
  109.5 27.7 %collective-permute-done = bf16[256,512]{1,0:T(8,128)(2,1)S(1)} collective-permute-done((bf16[256,512]{1,0:T(8,128)(2,1)S(1)}, bf16[256,512]{1,0:T(8,128)(2,1)S(1)}, u32[]{:S(2)}, u32[]{:S(2)}) %collective-permute-start) | collective-permute-done | bytes 262176 | tf_op jit(solution)/shard_map/ppermute | solution.py:400
  137.2 0.1 broadcast_in_dim.6
  137.4 0.1 convert_dynamic-update-slice_fusion.1
  137.4 0.0 copy-start
  137.4 5.3 %collective-permute-done.1 = bf16[256,512]{1,0:T(8,128)(2,1)S(1)} collective-permute-done((bf16[256,512]{1,0:T(8,128)(2,1)S(1)}, bf16[256,512]{1,0:T(8,128)(2,1)S(1)}, u32[]{:S(2)}, u32[]{:S(2)}) %collective-permute-start.1) | collective-permute-done | bytes 262176 | tf_op jit(solution)/shard_map/ppermute | solution.py:400
  142.8 0.0 copy-done
  142.8 0.9 convert_dynamic-update-slice_fusion
Async XLA Ops:
  5.4 99.4 %copy-start.2 = (s32[32]{0:T(128)S(1)}, s32[32]{0:T(128)}, u32[]{:S(2)}) copy-start(s32[32]{0:T(128)} %constant.90.clone) | copy-start | bytes 388
  5.4 101.3 %copy-start.1 = (s32[32]{0:T(128)S(1)}, s32[32]{0:T(128)}, u32[]{:S(2)}) copy-start(s32[32]{0:T(128)} %constant.91.clone) | copy-start | bytes 388
  101.9 35.3 %collective-permute-start = (bf16[256,512]{1,0:T(8,128)(2,1)S(1)}, bf16[256,512]{1,0:T(8,128)(2,1)S(1)}, u32[]{:S(2)}, u32[]{:S(2)}) collective-permute-start(bf16[256,512]{1,0:T(8,128)(2,1)S(1)} %get-tuple-element.6), channel_id=1, source_target_pairs={{0,0},{1,4},{2,8},{3,12},{4,16},{5,20},{6,24},{7,28},{8,1},{9,5},{... | collective-permute-start | bytes 786440 | tf_op jit(solution)/shard_map/ppermute | solution.py:400
  104.6 38.1 %collective-permute-start.1 = (bf16[256,512]{1,0:T(8,128)(2,1)S(1)}, bf16[256,512]{1,0:T(8,128)(2,1)S(1)}, u32[]{:S(2)}, u32[]{:S(2)}) collective-permute-start(bf16[256,512]{1,0:T(8,128)(2,1)S(1)} %get-tuple-element.5), channel_id=1, source_target_pairs={{0,4},{1,0},{2,12},{3,8},{4,20},{5,16},{6,28},{7,24},{8,5},{9,1},{... | collective-permute-start | bytes 786440 | tf_op jit(solution)/shard_map/ppermute | solution.py:400
  137.4 5.3 %copy-start = (f32[512,512]{1,0:T(8,128)}, f32[512,512]{1,0:T(8,128)S(1)}, u32[]{:S(2)}) copy-start(f32[512,512]{1,0:T(8,128)S(1)} %convert_dynamic-update-slice_fusion.1) | copy-start | bytes 3145732

commit v3 on v2

--- a/solution.py
+++ b/solution.py
@@ -18,6 +18,7 @@
 
 MESH = pl.DeviceIdType.MESH
 BLOCK = 256
+CUTS = 2
 
 
 def dot(a, b, dims=((1,), (0,))):
@@ -36,11 +37,11 @@
 
 def kernel(
     image, beam_hbm, counts_hbm, start, coarse_cos_hbm, coarse_sin_hbm, fine_cos, fine_sin,
-    sums,
+    out,
     column, coarse_cos, coarse_sin, beam, counts, strip, beamed, row_out, col_in, weighted, back_out, back_in,
-    real_in, imag_in, given, terms, starts, values, weight, sent, recv, mirror, first_out, first_in,
+    real_in, imag_in, given, terms, sums, pieces, starts, values, weight, sent, recv, mirror, first_out, first_in,
     load_sem, own_sem, image_send, image_recv, row_send, row_recv, back_send, back_recv,
-    layer_send, layer_recv, start_send, start_recv, count_sem,
+    layer_send, layer_recv, start_send, start_recv, piece_send, piece_recv, count_sem,
 ):
     parts, rows, tile = strip.shape
     layers, _, chunk = terms.shape
@@ -75,7 +76,24 @@
         pl.semaphore_signal(barrier, inc=1, device_id=(layer, peer(k)), device_id_type=MESH)
     for k in range(1, layers):
         pl.semaphore_signal(barrier, inc=1, device_id=(above(k), me), device_id_type=MESH)
-    pl.semaphore_wait(barrier, parts + layers - 2)
+    tall, broad, per_fold = out.shape[0] // rows, tile // chunk, points // tile
+    for a in range(tall):
+        for b in range(broad):
+            source = (lax.rem(me, per_fold) * broad + b, layer * tall + a)
+
+            @pl.when(jnp.logical_or(source[0] != layer, source[1] != me))
+            def _():
+                pl.semaphore_signal(barrier, inc=1, device_id=source, device_id_type=MESH)
+
+    def owner(f):
+        return lax.div(me, tall), f * per_fold + lax.div(layer, broad)
+
+    def is_mine(f):
+        q, c = owner(f)
+        return jnp.logical_and(q == layer, c == me)
+
+    local = sum(jnp.where(is_mine(f), 1, 0) for f in range(folds))
+    pl.semaphore_wait(barrier, parts + layers - 2 + folds - local)
 
     def image_copy(k):
         d = peer(k)
@@ -142,9 +160,20 @@
                 column[pl.ds(points + to, 16), at] = jnp.concatenate(sin_rows, 0).astype(jnp.bfloat16)
 
     loads[3].wait()
+
+    @pl.loop(0, rows // 8)
+    def _(g):
+        eight = pl.ds(pl.multiple_of(g * 8, 8), 8)
+        turned = beam[eight, :]
+        shift = jnp.broadcast_to(start[0:1, 0:1], (8, points))
+        step = 1
+        while step < points:
+            turned = jnp.where((shift & step) != 0, pltpu.roll(turned, step, 1), turned)
+            step *= 2
+        beam[eight, :] = turned
+
     mine.wait()
     origin = start[0:1, 0:1]
-    per_fold = points // tile
     for t in range(per_fold):
         for f in range(folds):
             src = t + per_fold * f
@@ -247,75 +276,132 @@
         weighted[at, :] = (scale * (cos_part + sign * pltpu.roll(sin_part, half, 1))).astype(jnp.bfloat16)
         weighted[low, :] = (scale * (sin_part - sign * pltpu.roll(cos_part, half, 1))).astype(jnp.bfloat16)
 
-    def inverse(d):
-        upper = dot(column[rows_of(d), :], weighted[:points, :])
-        lower = dot(column[rows_of(d + parts), :], weighted[points:, :])
-        return (upper + lower).astype(jnp.bfloat16)
-
-    def back_copy(k):
+    cut = rows // CUTS
+
+    def cut_of(h):
+        return pl.ds(h * cut, cut)
+
+    def inverse(d, h):
+        at = pl.ds(pl.multiple_of(d * rows + h * cut, cut), cut)
+        low = pl.ds(pl.multiple_of((d + parts) * rows + h * cut, cut), cut)
+        upper = dot(column[at, :], weighted[:points, :])
+        return (upper + dot(column[low, :], weighted[points:, :])).astype(jnp.bfloat16)
+
+    def back_copy(k, h):
         d = peer(k)
-        return remote(back_out.at[d], back_in.at[me], back_send.at[k], back_recv.at[me], (layer, d))
-
-    @pl.loop(1, parts)
-    def _(k):
-        d = peer(k)
-        back_out[d] = inverse(d)
-        back_copy(k).start()
-
-    back_in[me] = inverse(me)
-    for k in range(1, parts):
-        src = lax.rem(me + parts - k, parts)
-        arrived(back_in.at[src], back_recv.at[src])
-    for d in range(parts // 2):
-        lower = back_in[d].astype(jnp.float32)
-        upper = back_in[parts - 1 - d].astype(jnp.float32)
-        at = pl.ds(d * wide, wide)
-        real_in[:, at] = jnp.where(lane < half, lower, pltpu.roll(upper, half, 1)).astype(jnp.bfloat16)
-        imag_in[:, at] = jnp.where(lane < half, pltpu.roll(lower, half, 1), upper).astype(jnp.bfloat16)
+        return remote(
+            back_out.at[d, cut_of(h), :], back_in.at[me, cut_of(h), :],
+            back_send.at[h * parts + k], back_recv.at[h * parts + me], (layer, d),
+        )
+
+    for h in range(CUTS):
+
+        @pl.loop(1, parts)
+        def _(k):
+            d = peer(k)
+            back_out[d, cut_of(h), :] = inverse(d, h)
+            back_copy(k, h).start()
+
+        back_in[me, cut_of(h), :] = inverse(me, h)
 
     def chunk_of(q):
         return pl.ds(pl.multiple_of(q * chunk, chunk), chunk)
 
-    def contribution(q):
-        pixels = dot(real_in[...], column[: points // 2, chunk_of(q)])
-        pixels += dot(imag_in[...], column[points : points + points // 2, chunk_of(q)])
-        middle = imag_in[:, 0:1].astype(jnp.float32)
-        _, at = grid((rows, chunk))
+    def contribution(q, h):
+        pixels = dot(real_in[cut_of(h), :], column[: points // 2, chunk_of(q)])
+        pixels += dot(imag_in[cut_of(h), :], column[points : points + points // 2, chunk_of(q)])
+        middle = imag_in[cut_of(h), 0:1].astype(jnp.float32)
+        _, at = grid((cut, chunk))
         pixels += jnp.where(lax.rem(at, 2) == 0, middle, -middle)
-        return (beam[:, chunk_of(q)] * pixels).astype(jnp.bfloat16)
-
-    def layer_copy(k):
+        return (beam[cut_of(h), chunk_of(q)] * pixels).astype(jnp.bfloat16)
+
+    def layer_copy(k, h):
         q = above(k)
-        return remote(given.at[q], terms.at[layer], layer_send.at[k], layer_recv.at[layer], (q, me))
-
-    @pl.loop(1, layers)
-    def _(k):
-        q = above(k)
-        given[q] = contribution(q)
-        layer_copy(k).start()
-
-    terms[layer] = contribution(layer)
-    for k in range(1, layers):
-        src = lax.rem(layer + layers - k, layers)
-        arrived(starts.at[src], start_recv.at[src])
-        arrived(terms.at[src], layer_recv.at[src])
-
-    place = lax.broadcasted_iota(jnp.int32, (rows, chunk), 1) + layer * chunk
-    for f in range(folds):
-        total = jnp.zeros((rows, chunk), jnp.float32)
-        for p in range(layers):
-            offset = place + f * points - starts[p][0:1, 0:1]
-            inside = (offset >= 0) & (offset < points)
-            total += jnp.where(inside, terms[p].astype(jnp.float32), 0.0)
-        sums[f] = total.astype(jnp.bfloat16)
+        return remote(
+            given.at[q, cut_of(h), :], terms.at[layer, cut_of(h), :],
+            layer_send.at[h * layers + k], layer_recv.at[h * layers + layer], (q, me),
+        )
+
+    _, lane = grid((cut, wide))
+    for h in range(CUTS):
+        for k in range(1, parts):
+            src = lax.rem(me + parts - k, parts)
+            arrived(back_in.at[src, cut_of(h), :], back_recv.at[h * parts + src])
+        for d in range(parts // 2):
+            lower = back_in[d, cut_of(h), :].astype(jnp.float32)
+            upper = back_in[parts - 1 - d, cut_of(h), :].astype(jnp.float32)
+            at = pl.ds(d * wide, wide)
+            real_in[cut_of(h), at] = jnp.where(lane < half, lower, pltpu.roll(upper, half, 1)).astype(jnp.bfloat16)
+            imag_in[cut_of(h), at] = jnp.where(lane < half, pltpu.roll(lower, half, 1), upper).astype(jnp.bfloat16)
+
+        @pl.loop(1, layers)
+        def _(k):
+            q = above(k)
+            given[q, cut_of(h), :] = contribution(q, h)
+            layer_copy(k, h).start()
+
+        terms[layer, cut_of(h), :] = contribution(layer, h)
+
+    slot = lax.rem(me, tall) * broad + lax.rem(layer, broad)
+    slots = tall * broad
+
+    def piece_copy(f, h):
+        return remote(
+            sums.at[f, cut_of(h), :], pieces.at[slot, cut_of(h), :],
+            piece_send.at[h * folds + f], piece_recv.at[h * slots + slot], owner(f),
+        )
+
+    place = lax.broadcasted_iota(jnp.int32, (cut, chunk), 1) + layer * chunk
+    for h in range(CUTS):
+        for k in range(1, layers):
+            src = lax.rem(layer + layers - k, layers)
+            if h == 0:
+                arrived(starts.at[src], start_recv.at[src])
+            arrived(terms.at[src, cut_of(h), :], layer_recv.at[h * layers + src])
+        for f in range(folds):
+            total = jnp.zeros((cut, chunk), jnp.float32)
+            for p in range(layers):
+                offset = place + f * points - starts[p][0:1, 0:1]
+                inside = (offset >= 0) & (offset < points)
+                total += jnp.where(inside, terms[p, cut_of(h), :].astype(jnp.float32), 0.0)
+            sums[f, cut_of(h), :] = total.astype(jnp.bfloat16)
+
+            @pl.when(is_mine(f))
+            def _():
+                pieces[slot, cut_of(h), :] = sums[f, cut_of(h), :]
+
+            @pl.when(jnp.logical_not(is_mine(f)))
+            def _():
+                piece_copy(f, h).start()
+
+    for h in range(CUTS):
+        for a in range(tall):
+            for b in range(broad):
+                q, c = lax.rem(me, per_fold) * broad + b, layer * tall + a
+
+                @pl.when(jnp.logical_or(q != layer, c != me))
+                def _():
+                    at = a * broad + b
+                    arrived(pieces.at[at, cut_of(h), :], piece_recv.at[h * slots + at])
+
+                to = pl.ds(a * rows + h * cut, cut)
+                out[to, pl.ds(b * chunk, chunk)] = pieces[a * broad + b, cut_of(h), :].astype(jnp.float32)
 
     for k in range(1, parts):
         image_copy(k).wait_send()
-        back_copy(k).wait_send()
+        for h in range(CUTS):
+            back_copy(k, h).wait_send()
         row_copy(peer(k)).wait_send()
     for k in range(1, layers):
         start_copy(k).wait_send()
-        layer_copy(k).wait_send()
+        for h in range(CUTS):
+            layer_copy(k, h).wait_send()
+    for f in range(folds):
+
+        @pl.when(jnp.logical_not(is_mine(f)))
+        def _():
+            for h in range(CUTS):
+                piece_copy(f, h).wait_send()
 
 
 def strips(image, beam, counts, start, layers):
@@ -326,12 +412,13 @@
     chunk = points // layers
     coarse_cos, coarse_sin, fine_cos, fine_sin = (jnp.asarray(t) for t in make_tables(points))
     hp = max(wide // 2, 128)
+    slots = points // layers // rows * (tile // chunk)
     vmem, hbm = pl.BlockSpec(memory_space=pltpu.VMEM), pl.BlockSpec(memory_space=pl.ANY)
     bf = jnp.bfloat16
     dma = pltpu.SemaphoreType.DMA
     return pl.pallas_call(
         kernel,
-        out_shape=jax.ShapeDtypeStruct((folds, rows, chunk), bf),
+        out_shape=jax.ShapeDtypeStruct((points // layers, tile), jnp.float32),
         in_specs=[hbm, hbm, hbm, vmem, hbm, hbm, vmem, vmem],
         out_specs=vmem,
         scratch_shapes=[
@@ -351,6 +438,8 @@
             pltpu.VMEM((rows, points // 2), bf),
             pltpu.VMEM((layers, rows, chunk), bf),
             pltpu.VMEM((layers, rows, chunk), bf),
+            pltpu.VMEM((folds, rows, chunk), bf),
+            pltpu.VMEM((slots, rows, chunk), bf),
             pltpu.VMEM((layers, 8, 128), jnp.int32),
             pltpu.VMEM((points, wide), bf),
             pltpu.VMEM((points, wide), bf),
@@ -360,8 +449,8 @@
             pltpu.VMEM((16, points), bf),
             pltpu.VMEM((16, points), bf),
             dma((4,)), dma(()), dma((parts,)), dma((parts,)), dma((parts,)), dma((parts,)),
-            dma((parts,)), dma((parts,)), dma((layers,)), dma((layers,)), dma((layers,)), dma((layers,)),
-            dma((4,)),
+            dma((CUTS * parts,)), dma((CUTS * parts,)), dma((CUTS * layers,)), dma((CUTS * layers,)),
+            dma((layers,)), dma((layers,)), dma((CUTS * folds,)), dma((CUTS * slots,)), dma((4,)),
         ],
         compiler_params=pltpu.CompilerParams(
             collective_id=0, has_side_effects=True, vmem_limit_bytes=60 * 1024 * 1024
@@ -370,39 +459,8 @@
 
 
 def shards(image, beam, counts, offsets):
-    points = counts.shape[1]
-    parts, layers = lax.axis_size("img"), lax.axis_size("ptg")
-    me, layer = lax.axis_index("img"), lax.axis_index("ptg")
-    tile = image.shape[1]
-    folds = tile * parts // points
-    rows = points // parts
-    chunk = points // layers
-    start = offsets[0]
-    twice = jnp.concatenate([beam[0], beam[0]], 1)
-    rolled = lax.dynamic_slice_in_dim(twice, points - start % points, points, 1)
-    sums = strips(image, rolled, counts[0], jnp.full((8, 128), start, jnp.int32), layers)
-
-    out_rows = points // layers
-    tall, broad = out_rows // rows, tile // chunk
-    out = jnp.zeros((out_rows, tile), jnp.float32)
-    for s in range(folds):
-        pairs = []
-        row_at = np.zeros((layers * parts,), np.int32)
-        col_at = np.zeros((layers * parts,), np.int32)
-        for p in range(layers):
-            for i in range(parts):
-                f = (i % tall * broad + p % broad + s) % folds
-                q, c = i * rows // out_rows, (points * f + chunk * p) // tile
-                pairs.append((p * parts + i, q * parts + c))
-                row_at[q * parts + c] = i * rows - q * out_rows
-                col_at[q * parts + c] = points * f + chunk * p - tile * c
-        piece = lax.dynamic_index_in_dim(sums, (me % tall * broad + layer % broad + s) % folds, 0, False)
-        piece = lax.ppermute(piece, ("ptg", "img"), pairs)
-        here = layer * parts + me
-        out = lax.dynamic_update_slice(
-            out, piece.astype(jnp.float32), (jnp.asarray(row_at)[here], jnp.asarray(col_at)[here])
-        )
-    return out
+    start = jnp.full((8, 128), offsets[0], jnp.int32)
+    return strips(image, beam[0], counts[0], start, lax.axis_size("ptg"))
 
 
 def solution(mesh):

time: 144 us -> 129 us (0.90)
  waiting for transfers between devices: 33 us -> 0 us
  Pallas kernels: 95.5 us -> 124 us
  other arithmetic: 5.01 us -> 0 us
  between operations: 4.39 us -> 0.66 us
  starting transfers between devices: 2.79 us -> 0 us
    ppermute x2 -> x0, waiting for transfers between devices: 33 us -> none  [shards(): piece = lax.ppermute(piece, ('ptg', 'img'), pairs)]
    pallas_call x1, Pallas kernels: 95.5 us -> 124 us  [strips(): pl.pallas_call(kernel, out_shape=jax.ShapeDtypeStruct((points // layers,...]
    concatenate x1 -> x0, other arithmetic: 4.09 us -> none  [shards(): twice = jnp.concatenate([beam[0], beam[0]], 1)]
    ppermute x2 -> x0, starting transfers between devices: 2.79 us -> none  [shards(): piece = lax.ppermute(piece, ('ptg', 'img'), pairs)]
    unnamed x6 -> x1, local copies, waits for them, and re-layouts: 0.01 us -> 2.26 us
  transfers between devices with their start and end apart: 2 -> 0, of which waited for: 2 -> 0; matrix products, arithmetic and copies ran while one was open for 1% -> 0% of each run, Pallas kernels for 0% -> 0%
where the time goes in v3:
time: 129 us; the launch traced here: 127 us
  Pallas kernels  124 us (96%)
  local copies, waits for them, and re-layouts  2.86 us (2%)
    pallas_call x1, Pallas kernels, strips(): pl.pallas_call(kernel, out_shape=jax.ShapeDtypeStruct((points // layers,...  124 us

profile of v3, /device:TPU:1, one launch (start us, length us, event | category | flops | bytes accessed | tf_op | source)
XLA Modules:
  0.0 127.2 jit_solution(7713875570384183201)
XLA Ops:
  0.7 0.6 broadcast_in_dim.3.start
  1.2 123.7 %shard_map.82 = f32[512,512]{1,0:T(8,128)} custom-call(bf16[2048,512]{1,0:T(8,128)(2,1)} %image.1, f32[256,2048]{1,0:T(8,128)} %bitcast.4, s32[2048,256]{1,0:T(8,128)} %bitcast.5, s32[8,128]{1,0:T(8,128)} %broadcast_in_dim.3.start, f32[256,2048]{1,0:T(8,128)} %constant.8.clone.coarse_cos_hbm, f32[256,2048]{1,0:T(8,128)} %constant.9.clone.coarse_sin_hbm, ...), custom_call_target="tpu_custom_call" | custom-call | tf_op jit(solution)/shard_map/pallas_call | solution.py:419
  124.9 2.3 %copy.11 = f32[512,512]{1,0:T(8,128)} copy(f32[512,512]{1,0:T(8,128)} %shard_map.82) | data formatting | bytes 2097152

commit v4 on v3

--- a/solution.py
+++ b/solution.py
@@ -95,15 +95,24 @@
     local = sum(jnp.where(is_mine(f), 1, 0) for f in range(folds))
     pl.semaphore_wait(barrier, parts + layers - 2 + folds - local)
 
-    def image_copy(k):
+    cut = rows // CUTS
+
+    def cut_of(h):
+        return pl.ds(h * cut, cut)
+
+    def image_copy(k, h):
         d = peer(k)
-        return remote(image.at[rows_of(d), :], strip.at[me], image_send.at[k], image_recv.at[me], (layer, d))
+        return remote(
+            image.at[pl.ds(pl.multiple_of(d * rows + h * cut, cut), cut), :], strip.at[me, cut_of(h), :],
+            image_send.at[h * parts + k], image_recv.at[h * parts + me], (layer, d),
+        )
 
     def start_copy(k):
         return remote(start, starts.at[layer], start_send.at[k], start_recv.at[layer], (above(k), me))
 
-    for k in range(1, parts):
-        image_copy(k).start()
+    for h in range(CUTS):
+        for k in range(1, parts):
+            image_copy(k, h).start()
     for k in range(1, layers):
         start_copy(k).start()
     starts[layer] = start[...]
@@ -161,7 +170,7 @@
 
     loads[3].wait()
 
-    @pl.loop(0, rows // 8)
+    @pl.loop(0, rows // 8, unroll=4)
     def _(g):
         eight = pl.ds(pl.multiple_of(g * 8, 8), 8)
         turned = beam[eight, :]
@@ -174,50 +183,58 @@
 
     mine.wait()
     origin = start[0:1, 0:1]
-    for t in range(per_fold):
-        for f in range(folds):
-            src = t + per_fold * f
-
-            @pl.when(src != me)
-            def _():
-                arrived(strip.at[src], image_recv.at[src])
-
-        place = lax.broadcasted_iota(jnp.int32, (rows, tile), 1) + t * tile
-        window = strip[t + per_fold * (folds - 1)].astype(jnp.float32)
-        for f in range(folds - 2, -1, -1):
-            window = jnp.where(place + f * points >= origin, strip[t + per_fold * f].astype(jnp.float32), window)
-        at = pl.ds(t * tile, tile)
-        beamed[:, at] = (beam[:, at] * window).astype(jnp.bfloat16)
+    def window_cut(h):
+        for t in range(per_fold):
+            for f in range(folds):
+                src = t + per_fold * f
+
+                @pl.when(src != me)
+                def _():
+                    arrived(strip.at[src, cut_of(h), :], image_recv.at[h * parts + src])
+
+            place = lax.broadcasted_iota(jnp.int32, (cut, tile), 1) + t * tile
+            window = strip[t + per_fold * (folds - 1), cut_of(h), :].astype(jnp.float32)
+            for f in range(folds - 2, -1, -1):
+                other = strip[t + per_fold * f, cut_of(h), :].astype(jnp.float32)
+                window = jnp.where(place + f * points >= origin, other, window)
+            at = pl.ds(t * tile, tile)
+            beamed[cut_of(h), at] = (beam[cut_of(h), at] * window).astype(jnp.bfloat16)
 
     def columns_of(d):
         return pl.ds(pl.multiple_of(d * wide, wide), wide)
 
-    def row_copy(d):
-        return remote(row_out.at[d], col_in.at[rows_of(me), :], row_send.at[d], row_recv.at[me], (layer, d))
-
-    _, j = grid((rows, points))
-    sides = jnp.where(lax.rem(j, 2) == 0, beamed[...].astype(jnp.float32), -beamed[...].astype(jnp.float32))
-    alternating = jnp.sum(sides, 1, keepdims=True)
-    _, lane = grid((rows, wide))
-
-    @pl.loop(0, parts // 2)
-    def _(step):
-        d = lax.rem(me + 1 + step, parts // 2)
-        real = dot(beamed[...], column[:points, columns_of(d)])
-        imag = dot(beamed[...], column[points:, columns_of(d)])
-        imag = jnp.where(jnp.logical_and(lane == 0, d == 0), alternating, imag)
-        lower = jnp.where(lane < half, real, pltpu.roll(imag, half, 1)).astype(jnp.bfloat16)
-        upper = jnp.where(lane < half, pltpu.roll(real, half, 1), imag).astype(jnp.bfloat16)
-        for to, block in ((d, lower), (parts - 1 - d, upper)):
-
-            @pl.when(to == me)
-            def _():
-                col_in[rows_of(me), :] = block
-
-            @pl.when(to != me)
-            def _():
-                row_out[to] = block
-                row_copy(to).start()
+    def row_copy(d, h):
+        to = pl.ds(pl.multiple_of(me * rows + h * cut, cut), cut)
+        return remote(
+            row_out.at[d, cut_of(h), :], col_in.at[to, :],
+            row_send.at[h * parts + d], row_recv.at[h * parts + me], (layer, d),
+        )
+
+    _, column_at = grid((cut, points))
+    _, lane = grid((cut, wide))
+    for h in range(CUTS):
+        window_cut(h)
+        pixels = beamed[cut_of(h), :].astype(jnp.float32)
+        alternating = jnp.sum(jnp.where(lax.rem(column_at, 2) == 0, pixels, -pixels), 1, keepdims=True)
+
+        @pl.loop(0, parts // 2)
+        def _(step):
+            d = lax.rem(me + 1 + step, parts // 2)
+            real = dot(beamed[cut_of(h), :], column[:points, columns_of(d)])
+            imag = dot(beamed[cut_of(h), :], column[points:, columns_of(d)])
+            imag = jnp.where(jnp.logical_and(lane == 0, d == 0), alternating, imag)
+            lower = jnp.where(lane < half, real, pltpu.roll(imag, half, 1)).astype(jnp.bfloat16)
+            upper = jnp.where(lane < half, pltpu.roll(real, half, 1), imag).astype(jnp.bfloat16)
+            for to, block in ((d, lower), (parts - 1 - d, upper)):
+
+                @pl.when(to == me)
+                def _():
+                    col_in[pl.ds(pl.multiple_of(me * rows + h * cut, cut), cut), :] = block
+
+                @pl.when(to != me)
+                def _():
+                    row_out[to, cut_of(h), :] = block
+                    row_copy(to, h).start()
 
     count_copy.wait()
     first_copy.wait()
@@ -248,13 +265,13 @@
     mirror[...] = dot(first_in[...], first_b, ((0,), (0,))).astype(jnp.bfloat16)
     weight[...] = dot(first_in[...], first_a, ((0,), (0,))).astype(jnp.bfloat16)
 
-    @pl.loop(0, steps)
+    @pl.loop(0, steps, unroll=4)
     def _(b):
         at = block_of(b)
         total = dot(recv[at, :], recv_b) + dot(values[at, :], own_b)
         mirror[at, :] = (mirror[at, :].astype(jnp.float32) + total).astype(jnp.bfloat16)
 
-    @pl.loop(0, steps)
+    @pl.loop(0, steps, unroll=4)
     def _(b):
         at = block_of(b)
         total = dot(flip, mirror[block_of(steps - 1 - b), :])
@@ -264,9 +281,11 @@
 
     for k in range(1, parts):
         src = lax.rem(me + parts - k, parts)
-        arrived(col_in.at[rows_of(src), :], row_recv.at[src])
-
-    @pl.loop(0, steps)
+        for h in range(CUTS):
+            at = pl.ds(pl.multiple_of(src * rows + h * cut, cut), cut)
+            arrived(col_in.at[at, :], row_recv.at[h * parts + src])
+
+    @pl.loop(0, steps, unroll=2)
     def _(b):
         at = block_of(b)
         low = block_of(b + steps)
@@ -276,11 +295,6 @@
         weighted[at, :] = (scale * (cos_part + sign * pltpu.roll(sin_part, half, 1))).astype(jnp.bfloat16)
         weighted[low, :] = (scale * (sin_part - sign * pltpu.roll(cos_part, half, 1))).astype(jnp.bfloat16)
 
-    cut = rows // CUTS
-
-    def cut_of(h):
-        return pl.ds(h * cut, cut)
-
     def inverse(d, h):
         at = pl.ds(pl.multiple_of(d * rows + h * cut, cut), cut)
         low = pl.ds(pl.multiple_of((d + parts) * rows + h * cut, cut), cut)
@@ -322,7 +336,6 @@
             layer_send.at[h * layers + k], layer_recv.at[h * layers + layer], (q, me),
         )
 
-    _, lane = grid((cut, wide))
     for h in range(CUTS):
         for k in range(1, parts):
             src = lax.rem(me + parts - k, parts)
@@ -385,13 +398,13 @@
                     arrived(pieces.at[at, cut_of(h), :], piece_recv.at[h * slots + at])
 
                 to = pl.ds(a * rows + h * cut, cut)
-                out[to, pl.ds(b * chunk, chunk)] = pieces[a * broad + b, cut_of(h), :].astype(jnp.float32)
+                out[to, pl.ds(b * chunk, chunk)] = pieces[a * broad + b, cut_of(h), :]
 
     for k in range(1, parts):
-        image_copy(k).wait_send()
         for h in range(CUTS):
+            image_copy(k, h).wait_send()
+            row_copy(peer(k), h).wait_send()
             back_copy(k, h).wait_send()
-        row_copy(peer(k)).wait_send()
     for k in range(1, layers):
         start_copy(k).wait_send()
         for h in range(CUTS):
@@ -418,7 +431,7 @@
     dma = pltpu.SemaphoreType.DMA
     return pl.pallas_call(
         kernel,
-        out_shape=jax.ShapeDtypeStruct((points // layers, tile), jnp.float32),
+        out_shape=jax.ShapeDtypeStruct((points // layers, tile), bf),
         in_specs=[hbm, hbm, hbm, vmem, hbm, hbm, vmem, vmem],
         out_specs=vmem,
         scratch_shapes=[
@@ -448,7 +461,7 @@
             pltpu.VMEM((points, wide), bf),
             pltpu.VMEM((16, points), bf),
             pltpu.VMEM((16, points), bf),
-            dma((4,)), dma(()), dma((parts,)), dma((parts,)), dma((parts,)), dma((parts,)),
+            dma((4,)), dma(()), dma((CUTS * parts,)), dma((CUTS * parts,)), dma((CUTS * parts,)), dma((CUTS * parts,)),
             dma((CUTS * parts,)), dma((CUTS * parts,)), dma((CUTS * layers,)), dma((CUTS * layers,)),
             dma((layers,)), dma((layers,)), dma((CUTS * folds,)), dma((CUTS * slots,)), dma((4,)),
         ],
@@ -460,7 +473,7 @@
 
 def shards(image, beam, counts, offsets):
     start = jnp.full((8, 128), offsets[0], jnp.int32)
-    return strips(image, beam[0], counts[0], start, lax.axis_size("ptg"))
+    return strips(image, beam[0], counts[0], start, lax.axis_size("ptg")).astype(jnp.float32)
 
 
 def solution(mesh):

time: 129 us -> 129 us (level)
  local copies, waits for them, and re-layouts: 2.86 us -> 0.59 us
  other arithmetic: 0 us -> 2.15 us
    unnamed x1 -> x0, local copies, waits for them, and re-layouts: 2.26 us -> none
    convert_element_type x0 -> x1, other arithmetic: none -> 2.15 us  [shards(): strips(image, beam[0], counts[0], start, lax.axis_size('ptg'))]
where the time goes in v4:
time: 129 us; the launch traced here: 127 us
  Pallas kernels  123 us (95%)
  other arithmetic  2.15 us (2%)
    pallas_call x1, Pallas kernels, strips(): pl.pallas_call(kernel, out_shape=jax.ShapeDtypeStruct((points // layers,...  123 us

profile of v4, /device:TPU:1, one launch (start us, length us, event | category | flops | bytes accessed | tf_op | source)
XLA Modules:
  0.0 126.6 jit_solution(9742801660639096193)
XLA Ops:
  0.7 0.6 broadcast_in_dim.3.start
  1.2 123.2 %shard_map.82 = bf16[512,512]{1,0:T(8,128)(2,1)} custom-call(bf16[2048,512]{1,0:T(8,128)(2,1)} %image.1, f32[256,2048]{1,0:T(8,128)} %bitcast.4, s32[2048,256]{1,0:T(8,128)} %bitcast.5, s32[8,128]{1,0:T(8,128)} %broadcast_in_dim.3.start, f32[256,2048]{1,0:T(8,128)} %constant.8.clone.coarse_cos_hbm, f32[256,2048]{1,0:T(8,128)} %constant.9.clone.coarse_sin_hbm, ...), custom_call_target="tpu_custom_call" | custom-call | tf_op jit(solution)/shard_map/pallas_call | solution.py:432
  124.5 2.1 %convert_element_type.3 = f32[512,512]{1,0:T(8,128)} convert(bf16[512,512]{1,0:T(8,128)(2,1)} %shard_map.82) | non-fusion elementwise | flops 262144 | bytes 1572864 | tf_op jit(solution)/shard_map/convert_element_type | solution.py:476

commit v5 on v4

--- a/solution.py
+++ b/solution.py
@@ -39,13 +39,12 @@
     image, beam_hbm, counts_hbm, start, coarse_cos_hbm, coarse_sin_hbm, fine_cos, fine_sin,
     out,
     column, coarse_cos, coarse_sin, beam, counts, strip, beamed, row_out, col_in, weighted, back_out, back_in,
-    real_in, imag_in, given, terms, sums, pieces, starts, values, weight, sent, recv, mirror, first_out, first_in,
+    real_in, imag_in, given, gathered, terms, sums, pieces, starts, values, weight, sent, recv, mirror, first_out, first_in,
     load_sem, own_sem, image_send, image_recv, row_send, row_recv, back_send, back_recv,
-    layer_send, layer_recv, start_send, start_recv, piece_send, piece_recv, count_sem,
+    give_send, give_recv, layer_send, layer_recv, start_send, start_recv, piece_send, piece_recv, count_sem,
 ):
     parts, rows, tile = strip.shape
-    layers, _, chunk = terms.shape
-    folds = sums.shape[0]
+    layers, folds, sub = terms.shape[1], sums.shape[1], terms.shape[3]
     points = rows * parts
     wide = counts.shape[1]
     half = wide // 2
@@ -76,25 +75,8 @@
         pl.semaphore_signal(barrier, inc=1, device_id=(layer, peer(k)), device_id_type=MESH)
     for k in range(1, layers):
         pl.semaphore_signal(barrier, inc=1, device_id=(above(k), me), device_id_type=MESH)
-    tall, broad, per_fold = out.shape[0] // rows, tile // chunk, points // tile
-    for a in range(tall):
-        for b in range(broad):
-            source = (lax.rem(me, per_fold) * broad + b, layer * tall + a)
-
-            @pl.when(jnp.logical_or(source[0] != layer, source[1] != me))
-            def _():
-                pl.semaphore_signal(barrier, inc=1, device_id=source, device_id_type=MESH)
-
-    def owner(f):
-        return lax.div(me, tall), f * per_fold + lax.div(layer, broad)
-
-    def is_mine(f):
-        q, c = owner(f)
-        return jnp.logical_and(q == layer, c == me)
-
-    local = sum(jnp.where(is_mine(f), 1, 0) for f in range(folds))
-    pl.semaphore_wait(barrier, parts + layers - 2 + folds - local)
-
+    pl.semaphore_wait(barrier, parts + layers - 2)
+    tall, per_fold = out.shape[0] // rows, points // tile
     cut = rows // CUTS
 
     def cut_of(h):
@@ -318,22 +300,19 @@
 
         back_in[me, cut_of(h), :] = inverse(me, h)
 
-    def chunk_of(q):
-        return pl.ds(pl.multiple_of(q * chunk, chunk), chunk)
-
-    def contribution(q, h):
-        pixels = dot(real_in[cut_of(h), :], column[: points // 2, chunk_of(q)])
-        pixels += dot(imag_in[cut_of(h), :], column[points : points + points // 2, chunk_of(q)])
+    def contribution(t, h):
+        at = pl.ds(pl.multiple_of(t * tile, tile), tile)
+        pixels = dot(real_in[cut_of(h), :], column[: points // 2, at])
+        pixels += dot(imag_in[cut_of(h), :], column[points : points + points // 2, at])
         middle = imag_in[cut_of(h), 0:1].astype(jnp.float32)
-        _, at = grid((cut, chunk))
-        pixels += jnp.where(lax.rem(at, 2) == 0, middle, -middle)
-        return (beam[cut_of(h), chunk_of(q)] * pixels).astype(jnp.bfloat16)
-
-    def layer_copy(k, h):
-        q = above(k)
-        return remote(
-            given.at[q, cut_of(h), :], terms.at[layer, cut_of(h), :],
-            layer_send.at[h * layers + k], layer_recv.at[h * layers + layer], (q, me),
+        _, place = grid((cut, tile))
+        pixels += jnp.where(lax.rem(place, 2) == 0, middle, -middle)
+        return (beam[cut_of(h), at] * pixels).astype(jnp.bfloat16)
+
+    def give_copy(c, h):
+        return remote(
+            given.at[h, c], gathered.at[h, me],
+            give_send.at[h * parts + c], give_recv.at[h * parts + me], (layer, c),
         )
 
     for h in range(CUTS):
@@ -347,71 +326,94 @@
             real_in[cut_of(h), at] = jnp.where(lane < half, lower, pltpu.roll(upper, half, 1)).astype(jnp.bfloat16)
             imag_in[cut_of(h), at] = jnp.where(lane < half, pltpu.roll(lower, half, 1), upper).astype(jnp.bfloat16)
 
-        @pl.loop(1, layers)
-        def _(k):
-            q = above(k)
-            given[q, cut_of(h), :] = contribution(q, h)
+        @pl.loop(0, per_fold)
+        def _(step):
+            t = lax.rem(me + 1 + step, per_fold)
+            block = contribution(t, h)
+            for f in range(folds):
+                c = t + per_fold * f
+                share = block[f * sub : (f + 1) * sub]
+
+                @pl.when(c == me)
+                def _():
+                    gathered[h, me] = share
+
+                @pl.when(c != me)
+                def _():
+                    given[h, c] = share
+                    give_copy(c, h).start()
+
+    def layer_copy(k, h):
+        q = above(k)
+        return remote(
+            gathered.at[h, pl.ds(q * tall, tall)], terms.at[h, layer],
+            layer_send.at[h * layers + k], layer_recv.at[h * layers + layer], (q, me),
+        )
+
+    for h in range(CUTS):
+        for k in range(1, parts):
+            src = lax.rem(me + parts - k, parts)
+            arrived(gathered.at[h, src], give_recv.at[h * parts + src])
+        for k in range(1, layers):
             layer_copy(k, h).start()
-
-        terms[layer, cut_of(h), :] = contribution(layer, h)
-
-    slot = lax.rem(me, tall) * broad + lax.rem(layer, broad)
-    slots = tall * broad
+        for a in range(tall):
+            terms[h, layer, a] = gathered[h, layer * tall + a]
+
+    my_tile, my_fold = lax.rem(me, per_fold), lax.div(me, per_fold)
 
     def piece_copy(f, h):
         return remote(
-            sums.at[f, cut_of(h), :], pieces.at[slot, cut_of(h), :],
-            piece_send.at[h * folds + f], piece_recv.at[h * slots + slot], owner(f),
-        )
-
-    place = lax.broadcasted_iota(jnp.int32, (cut, chunk), 1) + layer * chunk
+            sums.at[h, f], pieces.at[h, my_fold],
+            piece_send.at[h * folds + f], piece_recv.at[h * folds + my_fold], (layer, my_tile + per_fold * f),
+        )
+
+    place = lax.broadcasted_iota(jnp.int32, (sub, tile), 1) + my_tile * tile
     for h in range(CUTS):
         for k in range(1, layers):
             src = lax.rem(layer + layers - k, layers)
             if h == 0:
                 arrived(starts.at[src], start_recv.at[src])
-            arrived(terms.at[src, cut_of(h), :], layer_recv.at[h * layers + src])
+            arrived(terms.at[h, src], layer_recv.at[h * layers + src])
         for f in range(folds):
-            total = jnp.zeros((cut, chunk), jnp.float32)
-            for p in range(layers):
-                offset = place + f * points - starts[p][0:1, 0:1]
-                inside = (offset >= 0) & (offset < points)
-                total += jnp.where(inside, terms[p, cut_of(h), :].astype(jnp.float32), 0.0)
-            sums[f, cut_of(h), :] = total.astype(jnp.bfloat16)
-
-            @pl.when(is_mine(f))
+            for a in range(tall):
+                total = jnp.zeros((sub, tile), jnp.float32)
+                for p in range(layers):
+                    offset = place + f * points - starts[p][0:1, 0:1]
+                    inside = (offset >= 0) & (offset < points)
+                    total += jnp.where(inside, terms[h, p, a].astype(jnp.float32), 0.0)
+                sums[h, f, a] = total.astype(jnp.bfloat16)
+
+            @pl.when(my_fold == f)
             def _():
-                pieces[slot, cut_of(h), :] = sums[f, cut_of(h), :]
-
-            @pl.when(jnp.logical_not(is_mine(f)))
+                pieces[h, f] = sums[h, f]
+
+            @pl.when(my_fold != f)
             def _():
                 piece_copy(f, h).start()
 
     for h in range(CUTS):
-        for a in range(tall):
-            for b in range(broad):
-                q, c = lax.rem(me, per_fold) * broad + b, layer * tall + a
-
-                @pl.when(jnp.logical_or(q != layer, c != me))
-                def _():
-                    at = a * broad + b
-                    arrived(pieces.at[at, cut_of(h), :], piece_recv.at[h * slots + at])
-
-                to = pl.ds(a * rows + h * cut, cut)
-                out[to, pl.ds(b * chunk, chunk)] = pieces[a * broad + b, cut_of(h), :]
+        for f in range(folds):
+
+            @pl.when(my_fold != f)
+            def _():
+                arrived(pieces.at[h, f], piece_recv.at[h * folds + f])
+
+            for a in range(tall):
+                out[pl.ds(a * rows + h * cut + f * sub, sub), :] = pieces[h, f, a]
 
     for k in range(1, parts):
         for h in range(CUTS):
             image_copy(k, h).wait_send()
             row_copy(peer(k), h).wait_send()
             back_copy(k, h).wait_send()
+            give_copy(peer(k), h).wait_send()
     for k in range(1, layers):
         start_copy(k).wait_send()
         for h in range(CUTS):
             layer_copy(k, h).wait_send()
     for f in range(folds):
 
-        @pl.when(jnp.logical_not(is_mine(f)))
+        @pl.when(my_fold != f)
         def _():
             for h in range(CUTS):
                 piece_copy(f, h).wait_send()
@@ -422,10 +424,9 @@
     rows, tile = beam.shape[0], image.shape[1]
     parts = points // rows
     folds = tile * parts // points
-    chunk = points // layers
     coarse_cos, coarse_sin, fine_cos, fine_sin = (jnp.asarray(t) for t in make_tables(points))
     hp = max(wide // 2, 128)
-    slots = points // layers // rows * (tile // chunk)
+    tall, sub = points // layers // rows, rows // CUTS // folds
     vmem, hbm = pl.BlockSpec(memory_space=pltpu.VMEM), pl.BlockSpec(memory_space=pl.ANY)
     bf = jnp.bfloat16
     dma = pltpu.SemaphoreType.DMA
@@ -449,10 +450,11 @@
             pltpu.VMEM((parts, rows, wide), bf),
             pltpu.VMEM((rows, points // 2), bf),
             pltpu.VMEM((rows, points // 2), bf),
-            pltpu.VMEM((layers, rows, chunk), bf),
-            pltpu.VMEM((layers, rows, chunk), bf),
-            pltpu.VMEM((folds, rows, chunk), bf),
-            pltpu.VMEM((slots, rows, chunk), bf),
+            pltpu.VMEM((CUTS, parts, sub, tile), bf),
+            pltpu.VMEM((CUTS, parts, sub, tile), bf),
+            pltpu.VMEM((CUTS, layers, tall, sub, tile), bf),
+            pltpu.VMEM((CUTS, folds, tall, sub, tile), bf),
+            pltpu.VMEM((CUTS, folds, tall, sub, tile), bf),
             pltpu.VMEM((layers, 8, 128), jnp.int32),
             pltpu.VMEM((points, wide), bf),
             pltpu.VMEM((points, wide), bf),
@@ -462,8 +464,9 @@
             pltpu.VMEM((16, points), bf),
             pltpu.VMEM((16, points), bf),
             dma((4,)), dma(()), dma((CUTS * parts,)), dma((CUTS * parts,)), dma((CUTS * parts,)), dma((CUTS * parts,)),
-            dma((CUTS * parts,)), dma((CUTS * parts,)), dma((CUTS * layers,)), dma((CUTS * layers,)),
-            dma((layers,)), dma((layers,)), dma((CUTS * folds,)), dma((CUTS * slots,)), dma((4,)),
+            dma((CUTS * parts,)), dma((CUTS * parts,)), dma((CUTS * parts,)), dma((CUTS * parts,)),
+            dma((CUTS * layers,)), dma((CUTS * layers,)),
+            dma((layers,)), dma((layers,)), dma((CUTS * folds,)), dma((CUTS * folds,)), dma((4,)),
         ],
         compiler_params=pltpu.CompilerParams(
             collective_id=0, has_side_effects=True, vmem_limit_bytes=60 * 1024 * 1024

time: 129 us -> 113 us (0.88)
  Pallas kernels: 123 us -> 108 us
    pallas_call x1, Pallas kernels: 123 us -> 108 us  [strips(): pl.pallas_call(kernel, out_shape=jax.ShapeDtypeStruct((points // layers,...]
where the time goes in v5:
time: 113 us; the launch traced here: 111 us
  Pallas kernels  108 us (96%)
  other arithmetic  2.15 us (2%)
    pallas_call x1, Pallas kernels, strips(): pl.pallas_call(kernel, out_shape=jax.ShapeDtypeStruct((points // layers,...  108 us

profile of v5, /device:TPU:1, one launch (start us, length us, event | category | flops | bytes accessed | tf_op | source)
XLA Modules:
  0.0 111.4 jit_solution(12395082578551517067)
XLA Ops:
  0.7 0.6 broadcast_in_dim.3.start
  1.2 108.0 %shard_map.82 = bf16[512,512]{1,0:T(8,128)(2,1)} custom-call(bf16[2048,512]{1,0:T(8,128)(2,1)} %image.1, f32[256,2048]{1,0:T(8,128)} %bitcast.4, s32[2048,256]{1,0:T(8,128)} %bitcast.5, s32[8,128]{1,0:T(8,128)} %broadcast_in_dim.3.start, f32[256,2048]{1,0:T(8,128)} %constant.8.clone.coarse_cos_hbm, f32[256,2048]{1,0:T(8,128)} %constant.9.clone.coarse_sin_hbm, ...), custom_call_target="tpu_custom_call" | custom-call | tf_op jit(solution)/shard_map/pallas_call | solution.py:433
  109.2 2.1 %convert_element_type.3 = f32[512,512]{1,0:T(8,128)} convert(bf16[512,512]{1,0:T(8,128)(2,1)} %shard_map.82) | non-fusion elementwise | flops 262144 | bytes 1572864 | tf_op jit(solution)/shard_map/convert_element_type | solution.py:479
